TPU v7x, 256 devices: a whole 4x4x8 slice. The times are simulated.
256 devices in a mesh: seg: 16 (over x_lo, y, core), grp: 16 (over x_hi, z).
Axes of the slice: x: 4 (x_hi: 2, x_lo: 2; x = x_hi * 2 + x_lo), y: 4, z: 8, core: 2. Of those that a mesh axis runs over, the one named last changes fastest.
Arguments:
- strain: bfloat16 [32768, 1792], P(('seg', 'grp')), may hold values from -40 to 40
- counts: int32 [32768], P(('seg', 'grp')), may hold values from 448 to 1792, as said below
- working: int32 [32768], P(('seg', 'grp')), may hold values 0 or 1
- mixing: bfloat16 [2048, 2048], P('grp'), may hold values from -0.125 to 0.125
- owners: int32 [2], replicated, may hold values from 0 to 255
- offsets: int32 [2], replicated, may hold values from 0 to 64
Outputs:
- correlations: bfloat16 [2, 201, 64, 32768], P(None, None, None, ('seg', 'grp'))
Inputs may be any that keep to these rules, and one draw needn't show every extreme that they name: `counts`: some channel has 1792 valid samples in every draw.
All inputs are finite; a program needn't handle non-finite values. No bound on the sum of `working` on one device may be relied on, other than what follows from the above.
Results may differ from a plain program's by a relative error of at most 0.0058.
Values may be sent and summed in bfloat16 or wider, within the bound.
No kernel may reach another device: no remote copies, remote signals or barrier semaphores. Data moves between devices by JAX's collectives and lax.ppermute only.
A program may use at most 64 MiB of HBM per device.

v0:
```python
import jax
import jax.numpy as jnp
from jax import lax
from jax.sharding import PartitionSpec as P

SRC = 64
LAG = 100
ROUNDS = 2
LAGS = 201


epsilon = 1e-05


def broadcast(value, axis, source):
    kept = jnp.where(lax.axis_index(axis) == source, value, 0).astype(value.dtype)
    return lax.psum(kept, axis)


def deliver(sent_block, owner_index):
    arrived = broadcast(sent_block, ("seg", "grp"), owner_index)
    return arrived


def correlate(whitened, source):
    lag_bunch = 8
    lag_groups = -(-LAGS // lag_bunch)
    total_lags = lag_groups * lag_bunch
    samples = whitened.shape[1]
    norm_scale = 1.0 / float(samples) ** 0.5
    source_pad = jnp.pad(source, ((0, 0), (LAG, LAG + total_lags - LAGS)))

    def group_step(unused_state, group_index):
        first_lag = group_index * lag_bunch
        shifted = jnp.stack(
            [
                lax.dynamic_slice_in_dim(source_pad, first_lag + lag_step, samples, 1)
                for lag_step in range(lag_bunch)
            ]
        )
        products = jnp.einsum("ksn,cn->ksc", shifted, whitened, preferred_element_type=jnp.float32)
        return (unused_state, (products * norm_scale).astype(jnp.bfloat16))

    unused_state, stacked = lax.scan(
        group_step, jnp.zeros((), jnp.float32), jnp.arange(lag_groups, dtype=jnp.int32)
    )
    return stacked.reshape(total_lags, source.shape[0], whitened.shape[0])[:LAGS]


def on_device(strain, counts, working, mixing, owners, offsets):
    positions = lax.broadcasted_iota(jnp.int32, strain.shape, 1)
    usable = (positions < counts[:, None]) & (working[:, None] > 0)
    masked = jnp.where(usable, strain, jnp.zeros_like(strain))
    coupled = jnp.dot(
        mixing,
        lax.all_gather(masked, "grp", axis=0, tiled=True),
        preferred_element_type=jnp.float32,
    )
    filtered = jnp.where(usable, masked.astype(jnp.float32) - coupled, jnp.float32(0.0))
    sumsq = jnp.sum(filtered * filtered, axis=1)
    spread = jnp.sqrt(sumsq / counts.astype(jnp.float32) + epsilon)
    whitened = (filtered / spread[:, None]).astype(jnp.bfloat16)
    rounds_out = []
    for round_index in range(ROUNDS):
        owner_index = owners[round_index]
        row_offset = offsets[round_index]
        source = lax.dynamic_slice_in_dim(deliver(whitened, owner_index), row_offset, SRC, 0)
        rounds_out.append(correlate(whitened, source))
    return jnp.stack(rounds_out)


def solution(mesh):
    in_specs = (
        P(("seg", "grp"), None),
        P(("seg", "grp")),
        P(("seg", "grp")),
        P("grp", None),
        P(),
        P(),
    )
    out_specs = P(None, None, None, ("seg", "grp"))
    return jax.shard_map(
        on_device, mesh=mesh, in_specs=in_specs, out_specs=out_specs, check_vma=False
    )
```

profile of v0, /device:TPU:1, one launch (start us, length us, event | category | flops | bytes accessed | tf_op | source)
XLA Modules:
  0.0 625.1 jit_solution(427242176838092812)
XLA Ops:
  8.5 1.7 fusion.11
  12.1 135.9 %all-gather.2.cloned.1.call-done = bf16[2048,1792]{0,1:T(8,128)(2,1)} async-done(((bf16[128,1792]{0,1:T(8,128)(2,1)}), bf16[2048,1792]{0,1:T(8,128)(2,1)}) %all-gather.2.cloned.1.call-update) | async-done | bytes 7340048 | tf_op jit(solution)/shard_map/all_gather | solution.py:56
  148.0 5.3 multiply_reduce_fusion
  159.6 249.1 %all-reduce.5.cloned.1.call-done = (bf16[128,1792]{0,1:T(8,128)(2,1)}, bf16[128,1792]{0,1:T(8,128)(2,1)}) async-done(((bf16[128,1792]{0,1:T(8,128)(2,1)}, bf16[128,1792]{0,1:T(8,128)(2,1)}), (bf16[128,1792]{0,1:T(8,128)(2,1)}, bf16[128,1792]{0,1:T(8,128)(2,1)})) %all-reduce.5.cloned.1.call-update) | async-done | bytes 917520 | tf_op jit(solution)/shard_map/psum | solution.py:17
  408.7 1.5 constant_dynamic-slice_fusion
  410.7 2.6 broadcast.23.clone
  413.3 97.4 %while.25 = (s32[]{:T(128)}, bf16[26,8,64,128]{3,2,1,0:T(8,128)(2,1)}, s32[26]{0:T(128)S(1)}, bf16[64,1999]{1,0:T(8,128)(2,1)S(1)}, bf16[128,1792]{1,0:T(8,128)(...) while((s32[]{:T(128)}, ...), condition=%wide.region_6.7_spmd, body=%wide.region_5.6_spmd.sunk | while | flops 235012128 | bytes 6095469 | solution.py:44
  415.8 1.3 fusion.29
  419.5 1.3 fusion.29
  423.3 1.3 fusion.29
  427.0 1.3 fusion.29
  430.8 1.3 fusion.29
  434.5 1.3 fusion.29
  438.3 1.3 fusion.29
  442.0 1.3 fusion.29
  445.7 1.3 fusion.29
  449.5 1.3 fusion.29
  453.2 1.3 fusion.29
  457.0 1.3 fusion.29
  460.7 1.3 fusion.29
  464.5 1.3 fusion.29
  468.2 1.3 fusion.29
  472.0 1.3 fusion.29
  475.7 1.3 fusion.29
  479.4 1.3 fusion.29
  483.2 1.3 fusion.29
  486.9 1.3 fusion.29
  490.7 1.3 fusion.29
  494.4 1.3 fusion.29
  498.2 1.3 fusion.29
  501.9 1.3 fusion.29
  505.7 1.3 fusion.29
  509.4 1.3 fusion.29
  510.7 4.3 slice_bitcast_fusion
  515.2 2.6 broadcast.23.clone.1
  517.8 94.1 %while.24 = (s32[]{:T(128)}, bf16[26,8,64,128]{3,2,1,0:T(8,128)(2,1)}, s32[26]{0:T(128)S(1)}, bf16[64,1999]{1,0:T(8,128)(2,1)S(1)}, bf16[128,1792]{1,0:T(8,128)(...) while((s32[]{:T(128)}, ...), condition=%wide.region_3.4_spmd, body=%wide.region_2.3_spmd.sunk | while | flops 235012128 | bytes 6095469 | solution.py:44
  523.7 1.3 fusion.26
  527.4 1.3 fusion.26
  531.0 1.3 fusion.26
  534.6 1.3 fusion.26
  538.2 1.3 fusion.26
  541.9 1.3 fusion.26
  545.5 1.3 fusion.26
  549.1 1.3 fusion.26
  552.7 1.3 fusion.26
  556.3 1.3 fusion.26
  612.0 2.8 slice_bitcast_fusion.1
  614.9 3.4 pad_maximum_fusion
  (512 shorter events, 114.3 us)
Async XLA Ops:
  6.5 141.5 %copy-start = (bf16[128,2048]{1,0:T(8,128)(2,1)S(1)}, bf16[128,2048]{1,0:T(8,128)(2,1)}, u32[]{:S(2)}) copy-start(bf16[128,2048]{1,0:T(8,128)(2,1)} %param.13) | copy-start | bytes 1572868
  6.5 141.5 %copy-start.4 = (s32[128]{0:T(128)S(1)}, s32[128]{0:T(128)}, u32[]{:S(2)}) copy-start(s32[128]{0:T(128)} %param.11) | copy-start | bytes 1540
  6.5 3.8 copy-start.2
  6.5 141.5 %all-gather.2.cloned.1.call-start = ((), (), s32[]{:S(2)}) async-start(), calls=%async_computation | async-start | bytes 7798784 | tf_op jit(solution)/shard_map/all_gather | solution.py:56
  10.2 398.5 %all-reduce.5.cloned.1.call-start = ((), (), s32[]{:S(2)}) async-start(), calls=%async_computation.1 | async-start | bytes 1835008 | tf_op jit(solution)/shard_map/psum | solution.py:17
  153.3 1.8 copy-start.3
  612.0 2.9 copy-start.1
Sparse Core Ops, SparseCore 0:
  10.4 137.6 all-gather.1
  155.2 253.4 all-reduce.4
where the time goes:
time: 628 us; the launch traced here: 625 us
  waiting for transfers between devices  385 us (61%)
  local copies, waits for them, and re-layouts  105 us (17%)
  matrix products  72.9 us (12%)
  loops' own time  36.5 us (6%)
  between operations  18.4 us (3%)
  other arithmetic  7.49 us (1%)
    psum x1, waiting for transfers between devices, broadcast(): return lax.psum(kept, axis)  249 us
    all_gather x1, waiting for transfers between devices, on_device(): lax.all_gather(masked, 'grp', axis=0, tiled=True)  136 us
    dot_general x52, matrix products, group_step(): jnp.einsum('ksn,cn->ksc', shifted, whitened, preferred_element_type=jnp.f...  67.6 us
    while x364, local copies, waits for them, and re-layouts  49.9 us
    another operation x2, loops' own time, correlate(): lax.scan(group_step, jnp.zeros((), jnp.float32), jnp.arange(lag_groups, d...  36.5 us
    dynamic_slice x52, local copies, waits for them, and re-layouts, correlate(): lax.scan(group_step, jnp.zeros((), jnp.float32), jnp.arange(lag_groups, d...  30.4 us
  transfers between devices with their start and end apart: 2, of which 2 were waited for; matrix products, arithmetic and copies ran while one was open for 0% of the time, Pallas kernels for 0%

commit v1 on v0

v1 whole, which is shorter than its diff:
```python
import jax
import jax.numpy as jnp
from jax import lax
from jax.experimental import pallas as pl
from jax.experimental.pallas import tpu as pltpu
from jax.sharding import PartitionSpec as P

SRC = 64
LAG = 100
ROUNDS = 2
LAGS = 201
DEPTH = 8
FINE = 13
COARSE = 8
PAIR = 2

epsilon = 1e-05

ACROSS = [(a * DEPTH + z, (1 - a) * DEPTH + z) for a in range(2) for z in range(DEPTH)]
UP = [(a * DEPTH + z, a * DEPTH + (z + 1) % DEPTH) for a in range(2) for z in range(DEPTH)]
DOWN = [(a * DEPTH + z, a * DEPTH + (z - 1) % DEPTH) for a in range(2) for z in range(DEPTH)]


def correlate_kernel(channel_ref, source_ref, out_ref, turned_ref, left_ref, right_ref):
    step = pl.program_id(0)
    rows, samples = source_ref.shape
    channels = channel_ref.shape[0]
    span = FINE * COARSE
    half_steps = COARSE // PAIR

    @pl.when(step == 0)
    def _():
        turned_ref[...] = jnp.zeros_like(turned_ref)
        turned_ref[span : span + samples, :] = channel_ref[...].astype(jnp.float32).T

    def build(first):
        padded = jnp.concatenate(
            [source_ref[...].astype(jnp.float32), jnp.zeros((rows, 128), jnp.float32)], axis=1
        )
        for fine in range(FINE):
            ahead = first + fine
            moved = pltpu.roll(padded, (-ahead) % (samples + 128), axis=1) if ahead else padded
            left_ref[fine * rows : (fine + 1) * rows, :] = moved[:, :samples].astype(jnp.bfloat16)

    @pl.when(step == 0)
    def _():
        build(1 - FINE)

    @pl.when(step == half_steps)
    def _():
        build(1)

    low = step < half_steps
    part = lax.rem(step, half_steps)
    for half in range(PAIR):
        coarse = FINE * (part * PAIR + half)
        start = jnp.where(low, span + coarse, span - coarse)
        right_ref[:, half * channels : (half + 1) * channels] = turned_ref[
            pl.ds(start, samples), :
        ].astype(jnp.bfloat16)
    products = jnp.dot(left_ref[...], right_ref[...], preferred_element_type=jnp.float32)
    scaled = (products * (1.0 / float(samples) ** 0.5)).astype(jnp.bfloat16)
    for half in range(PAIR):
        coarse = FINE * (part * PAIR + half)
        first = jnp.where(low, LAG + 1 - FINE - coarse, LAG + 1 + coarse)
        for fine in range(FINE):
            lag = first + fine

            @pl.when((lag >= 0) & (lag < LAGS))
            def _():
                for r in range(ROUNDS):
                    top = fine * rows + r * SRC
                    out_ref[r, lag] = scaled[top : top + SRC, half * channels : (half + 1) * channels]


def correlate(whitened, sources):
    channels, samples = whitened.shape
    rows = sources.shape[0]
    span = FINE * COARSE
    return pl.pallas_call(
        correlate_kernel,
        grid=(2 * COARSE // PAIR,),
        out_shape=jax.ShapeDtypeStruct((ROUNDS, LAGS, SRC, channels), jnp.bfloat16),
        in_specs=[
            pl.BlockSpec((channels, samples), lambda i: (0, 0)),
            pl.BlockSpec((rows, samples), lambda i: (0, 0)),
        ],
        out_specs=pl.BlockSpec((ROUNDS, LAGS, SRC, channels), lambda i: (0, 0, 0, 0)),
        scratch_shapes=[
            pltpu.VMEM((samples + 2 * span, channels), jnp.float32),
            pltpu.VMEM((FINE * rows, samples), jnp.bfloat16),
            pltpu.VMEM((samples, PAIR * channels), jnp.bfloat16),
        ],
        compiler_params=pltpu.CompilerParams(vmem_limit_bytes=56 * 2**20),
        cost_estimate=pl.CostEstimate(
            flops=2 * LAGS * rows * channels * samples, bytes_accessed=8 * 2**20, transcendentals=0
        ),
    )(whitened, sources)


def everyone(block, axis):
    copies = lax.axis_size(axis)
    tiled = jnp.broadcast_to(block[None], (copies,) + block.shape)
    return lax.all_to_all(tiled, axis, 0, 0)


def on_device(strain, counts, working, mixing, owners, offsets):
    channels, samples = strain.shape
    part = samples // 2
    seg = lax.axis_index("seg")
    grp = lax.axis_index("grp")
    side, level = grp // DEPTH, grp % DEPTH

    facts = jnp.stack([counts, working])
    facts = jnp.concatenate([facts, lax.ppermute(facts, "grp", ACROSS)], axis=1)
    counts2, working2 = facts[0], facts[1]
    positions = lax.broadcasted_iota(jnp.int32, strain.shape, 1)
    usable = (positions < counts[:, None]) & (working[:, None] > 0)
    masked = jnp.where(usable, strain, jnp.zeros_like(strain))
    first, second = masked[:, :part], masked[:, part:]
    mine = jnp.where(side == 0, first, second)
    theirs = jnp.where(side == 0, second, first)
    block = jnp.concatenate([mine, lax.ppermute(theirs, "grp", ACROSS)])
    mixing2 = jnp.concatenate([mixing, lax.ppermute(mixing, "grp", ACROSS)])

    def weights(away, who):
        at = (jnp.where(who == 0, side, 1 - side) * DEPTH + (level + away) % DEPTH) * channels
        return lax.dynamic_slice_in_dim(mixing2, at, channels, 1)

    def term(away, rows, who=None):
        if who is None:
            left = jnp.concatenate([weights(away, 0), weights(away, 1)], axis=1)
        else:
            left = weights(away, who)
        return jnp.dot(left, rows, preferred_element_type=jnp.float32)

    coupled = term(0, block)
    up, down = block, block
    for hop in range(1, DEPTH // 2):
        up = lax.ppermute(up, "grp", UP)
        down = lax.ppermute(down, "grp", DOWN)
        coupled = coupled + term(-hop, up) + term(hop, down)
    up = lax.ppermute(up[:channels], "grp", UP)
    down = lax.ppermute(down[channels:], "grp", DOWN)
    coupled = coupled + term(DEPTH // 2, up, 0) + term(DEPTH // 2, down, 1)

    places = side * part + lax.broadcasted_iota(jnp.int32, block.shape, 1)
    usable2 = (places < counts2[:, None]) & (working2[:, None] > 0)
    filtered = jnp.where(usable2, block.astype(jnp.float32) - coupled, jnp.float32(0.0))
    sums = jnp.sum(filtered * filtered, axis=1)
    sums = sums + jnp.roll(lax.ppermute(sums, "grp", ACROSS), channels)
    spread = jnp.sqrt(sums / counts2.astype(jnp.float32) + epsilon)
    white = (filtered / spread[:, None]).astype(jnp.bfloat16)

    returned = lax.ppermute(white[channels:], "grp", ACROSS)
    picked = []
    for r in range(ROUNDS):
        owner_seg, owner_grp = owners[r] // 16, owners[r] % 16
        row = jnp.where(owner_grp // DEPTH == side, 0, channels) + offsets[r]
        rows = lax.dynamic_slice_in_dim(white, row, SRC, 0)
        here = (owner_seg == seg) & (owner_grp % DEPTH == level)
        picked.append(jnp.where(here, rows, jnp.zeros_like(rows)))
    segs = lax.axis_size("seg")
    sources = jnp.concatenate(picked).reshape(segs, ROUNDS * SRC // segs, part)
    sources = jnp.sum(lax.all_to_all(sources, "seg", 0, 0), axis=0)
    sources = everyone(sources, "grp").reshape(2, DEPTH, ROUNDS * SRC // segs, part)
    sources = jnp.sum(sources, axis=1)
    sources = jnp.concatenate([sources[0], sources[1]], axis=1)
    sources = everyone(sources, "seg").reshape(ROUNDS * SRC, samples)

    kept = white[:channels]
    whitened = jnp.concatenate(
        [jnp.where(side == 0, kept, returned), jnp.where(side == 0, returned, kept)], axis=1
    )
    return correlate(whitened, sources)


def solution(mesh):
    in_specs = (
        P(("seg", "grp"), None),
        P(("seg", "grp")),
        P(("seg", "grp")),
        P("grp", None),
        P(),
        P(),
    )
    out_specs = P(None, None, None, ("seg", "grp"))
    return jax.shard_map(
        on_device, mesh=mesh, in_specs=in_specs, out_specs=out_specs, check_vma=False
    )
```

time: 628 us -> 148 us (0.24)
  waiting for transfers between devices: 385 us -> 41.9 us
  local copies, waits for them, and re-layouts: 105 us -> 6.38 us
  matrix products: 72.9 us -> 3.04 us
  starting transfers between devices: 0.04 us -> 42.1 us
  loops' own time: 36.5 us -> 0 us
  Pallas kernels: 0 us -> 23.4 us
  blocking collectives: 0 us -> 19 us
  between operations: 18.4 us -> 6.73 us
    psum x1 -> x0, waiting for transfers between devices: 249 us -> none  [broadcast(): return lax.psum(kept, axis)]
    all_gather x1 -> x0, waiting for transfers between devices: 136 us -> none  [on_device(): lax.all_gather(masked, 'grp', axis=0, tiled=True)]
    dot_general x53 -> x9, matrix products: 72.9 us -> 3.04 us  [term(): return jnp.dot(left, rows, preferred_element_type=jnp.float32)]
    while x365 -> x0, local copies, waits for them, and re-layouts: 50.1 us -> none
    another operation x2 -> x0, loops' own time: 36.5 us -> none  [correlate(): lax.scan(group_step, jnp.zeros((), jnp.float32), jnp.arange(lag_groups, d...]
    dynamic_slice x53 -> x1, local copies, waits for them, and re-layouts: 31.9 us -> 0.27 us  [weights(): return lax.dynamic_slice_in_dim(mixing2, at, channels, 1)]
    ppermute x0 -> x13, starting transfers between devices: none -> 28.4 us  [the longest x3 10.8 us: on_device(): down = lax.ppermute(down, 'grp', DOWN)]
    ppermute x0 -> x13, waiting for transfers between devices: none -> 27.6 us  [the longest x3 14.2 us: on_device(): down = lax.ppermute(down, 'grp', DOWN)]
  transfers between devices with their start and end apart: 2 -> 15, of which waited for: 2 -> 7; matrix products, arithmetic and copies ran while one was open for 0% -> 8% of each run, Pallas kernels for 0% -> 0%
where the time goes in v1:
time: 148 us; the launch traced here: 147 us
  starting transfers between devices  42.1 us (28%)
  waiting for transfers between devices  41.9 us (28%)
  Pallas kernels  23.4 us (16%)
  blocking collectives  19 us (13%)
  between operations  6.73 us (5%)
  local copies, waits for them, and re-layouts  6.38 us (4%)
  other arithmetic  4.71 us (3%)
  matrix products  3.04 us (2%)
    pallas_call x1, Pallas kernels, correlate(): pl.pallas_call(correlate_kernel, grid=(2 * COARSE // PAIR,), out_shape=ja...  23.4 us
    all_to_all x1, blocking collectives, on_device(): sources = jnp.sum(lax.all_to_all(sources, 'seg', 0, 0), axis=0)  19 us
    all_to_all x2, waiting for transfers between devices, everyone(): return lax.all_to_all(tiled, axis, 0, 0)  14.4 us
    ppermute x3, waiting for transfers between devices, on_device(): down = lax.ppermute(down, 'grp', DOWN)  14.2 us
    all_to_all x2, starting transfers between devices, everyone(): return lax.all_to_all(tiled, axis, 0, 0)  13.7 us
    ppermute x3, starting transfers between devices, on_device(): down = lax.ppermute(down, 'grp', DOWN)  10.8 us
    ppermute x3, waiting for transfers between devices, on_device(): up = lax.ppermute(up, 'grp', UP)  8.89 us
    ppermute x1, starting transfers between devices, on_device(): mixing2 = jnp.concatenate([mixing, lax.ppermute(mixing, 'grp', ACROSS)])  3.57 us
  transfers between devices with their start and end apart: 15, of which 7 were waited for; matrix products, arithmetic and copies ran while one was open for 8% of the time, Pallas kernels for 0%

profile of v1, /device:TPU:1, one launch (start us, length us, event | category | flops | bytes accessed | tf_op | source)
XLA Modules:
  0.0 147.3 jit_solution(12243598584757418396)
XLA Ops:
  0.0 3.6 %collective-permute-start.2 = (bf16[128,2048]{1,0:T(8,128)(2,1)}, bf16[128,2048]{1,0:T(8,128)(2,1)S(1)}, u32[]{:S(2)}, u32[]{:S(2)}) collective-permute-start(bf16[128,2048]{1,0:T(8,128)(2,1)} %param.9), channel_id=1, source_target_pairs={{0,8},{1,9},{2,10},{3,11},{4,12},{5,13},{6,14},{7,15},{8,0},{9,1},... | collective-permute-start | bytes 1572872 | tf_op jit(solution)/shard_map/ppermute | solution.py:124
  3.6 0.7 broadcast_compare_fusion
  4.2 1.4 fusion.8
  5.6 0.1 broadcast_select_fusion.3
  5.7 0.1 collective-permute-start.1
  5.8 0.7 pad_add_fusion.1
  6.5 3.0 %collective-permute-start = (s32[2,128]{1,0:T(2,128)S(1)}, s32[2,128]{1,0:T(2,128)S(1)}, u32[]{:S(2)}, u32[]{:S(2)}) collective-permute-start(s32[2,128]{1,0:T(2,128)S(1)} %pad_add_fusion.1), channel_id=1, source_target_pairs={{0,8},{1,9},{2,10},{3,11},{4,12},{5,13},{6,14},{7,15},{8,0},{9,1},... | collective-permute-start | bytes 3080 | tf_op jit(solution)/shard_map/ppermute | solution.py:115
  9.4 1.1 constant_dynamic-update-slice_fusion.1
  10.5 1.4 fusion.50
  13.2 1.3 fusion.49
  19.7 0.7 pad_add_fusion
  20.4 2.3 %collective-permute-start.3 = (bf16[256,896]{1,0:T(8,128)(2,1)S(1)}, bf16[256,896]{1,0:T(8,128)(2,1)S(1)}, u32[]{:S(2)}, u32[]{:S(2)}) collective-permute-start(bf16[256,896]{1,0:T(8,128)(2,1)S(1)} %pad_maximum_fusion), channel_id=1, source_target_pairs={{0,1},{1,2},{2,3},{3,4},{4,5},{5,6},{6,7},{7,0},{8,9},{9,10},{10,1... | collective-permute-start | bytes 1376264 | tf_op jit(solution)/shard_map/ppermute | solution.py:140
  22.7 4.0 %collective-permute-start.4 = (bf16[256,896]{1,0:T(8,128)(2,1)S(1)}, bf16[256,896]{1,0:T(8,128)(2,1)S(1)}, u32[]{:S(2)}, u32[]{:S(2)}) collective-permute-start(bf16[256,896]{1,0:T(8,128)(2,1)S(1)} %pad_maximum_fusion), channel_id=1, source_target_pairs={{0,7},{1,0},{2,1},{3,2},{4,3},{5,4},{6,5},{7,6},{8,15},{9,8},{10,9... | collective-permute-start | bytes 1376264 | tf_op jit(solution)/shard_map/ppermute | solution.py:141
  26.8 0.3 constant_dynamic-slice_fusion.3
  27.1 7.9 %collective-permute-done.4 = bf16[256,896]{1,0:T(8,128)(2,1)S(1)} collective-permute-done((bf16[256,896]{1,0:T(8,128)(2,1)S(1)}, bf16[256,896]{1,0:T(8,128)(2,1)S(1)}, u32[]{:S(2)}, u32[]{:S(2)}) %collective-permute-start.4) | collective-permute-done | bytes 458784 | tf_op jit(solution)/shard_map/ppermute | solution.py:141
  35.0 3.4 %collective-permute-start.6 = (bf16[256,896]{1,0:T(8,128)(2,1)S(1)}, bf16[256,896]{1,0:T(8,128)(2,1)S(1)}, u32[]{:S(2)}, u32[]{:S(2)}) collective-permute-start(bf16[256,896]{1,0:T(8,128)(2,1)S(1)} %collective-permute-done.4), channel_id=1, source_target_pairs={{0,7},{1,0},{2,1},{3,2},{4,3},{5,4},{6,5},{7,6},{8,15},{9,8},{10,9... | collective-permute-start | bytes 1376264 | tf_op jit(solution)/shard_map/ppermute | solution.py:141
  38.4 0.0 collective-permute-done.3
  38.4 0.3 fusion.12
  38.7 0.3 fusion.16
  39.0 0.3 fusion.5
  39.3 6.4 %collective-permute-done.6 = bf16[256,896]{1,0:T(8,128)(2,1)S(1)} collective-permute-done((bf16[256,896]{1,0:T(8,128)(2,1)S(1)}, bf16[256,896]{1,0:T(8,128)(2,1)S(1)}, u32[]{:S(2)}, u32[]{:S(2)}) %collective-permute-start.6) | collective-permute-done | bytes 458784 | tf_op jit(solution)/shard_map/ppermute | solution.py:141
  45.7 3.4 %collective-permute-start.8 = (bf16[256,896]{1,0:T(8,128)(2,1)S(1)}, bf16[256,896]{1,0:T(8,128)(2,1)S(1)}, u32[]{:S(2)}, u32[]{:S(2)}) collective-permute-start(bf16[256,896]{1,0:T(8,128)(2,1)S(1)} %collective-permute-done.6), channel_id=1, source_target_pairs={{0,7},{1,0},{2,1},{3,2},{4,3},{5,4},{6,5},{7,6},{8,15},{9,8},{10,9... | collective-permute-start | bytes 1376264 | tf_op jit(solution)/shard_map/ppermute | solution.py:141
  49.1 0.3 fusion.23
  49.4 0.3 fusion.4
  49.7 8.9 %collective-permute-done.7 = bf16[256,896]{1,0:T(8,128)(2,1)S(1)} collective-permute-done((bf16[256,896]{1,0:T(8,128)(2,1)S(1)}, bf16[256,896]{1,0:T(8,128)(2,1)S(1)}, u32[]{:S(2)}, u32[]{:S(2)}) %collective-permute-start.7) | collective-permute-done | bytes 458784 | tf_op jit(solution)/shard_map/ppermute | solution.py:140
  58.6 0.1 collective-permute-start.9
  58.8 2.7 %collective-permute-start.10 = (bf16[128,896]{1,0:T(8,128)(2,1)S(1)}, bf16[128,896]{1,0:T(8,128)(2,1)S(1)}, u32[]{:S(2)}, u32[]{:S(2)}) collective-permute-start(bf16[128,896]{1,0:T(8,128)(2,1)S(1)} %slice.73), channel_id=1, source_target_pairs={{0,7},{1,0},{2,1},{3,2},{4,3},{5,4},{6,5},{7,6},{8,15},{9,8},{10,9... | collective-permute-start | bytes 688136 | tf_op jit(solution)/shard_map/ppermute | solution.py:144
  61.5 0.3 fusion.30
  61.8 3.2 %collective-permute-done.9 = bf16[128,896]{1,0:T(8,128)(2,1)S(1)} collective-permute-done((bf16[128,896]{1,0:T(8,128)(2,1)S(1)}, bf16[128,896]{1,0:T(8,128)(2,1)S(1)}, u32[]{:S(2)}, u32[]{:S(2)}) %collective-permute-start.9) | collective-permute-done | bytes 229408 | tf_op jit(solution)/shard_map/ppermute | solution.py:143
  65.0 0.3 fusion.36
  65.3 0.3 fusion.34
  65.6 0.7 multiply_reduce_fusion
  66.3 2.8 %collective-permute-start.11 = (f32[256]{0:T(256)S(1)}, f32[256]{0:T(256)S(1)}, u32[]{:S(2)}, u32[]{:S(2)}) collective-permute-start(f32[256]{0:T(256)S(1)} %get-tuple-element.33), channel_id=1, source_target_pairs={{0,8},{1,9},{2,10},{3,11},{4,12},{5,13},{6,14},{7,15},{8,0},{9,1},... | collective-permute-start | bytes 3080 | tf_op jit(solution)/shard_map/ppermute | solution.py:151
  69.1 1.2 collective-permute-done.11
  70.3 0.1 divide_convert_fusion
  70.4 0.1 dynamic-slice_select_fusion.1
  70.6 19.0 %all_to_all.15 = bf16[16,8,896]{2,1,0:T(8,128)(2,1)S(1)} all-to-all(bf16[16,8,896]{2,1,0:T(8,128)(2,1)S(1)} %maximum_bitcast_fusion), channel_id=1, replica_groups=mesh['seg'=16,'grp'=16] {'seg'}, dimensions={0} | all-to-all | bytes 458752 | tf_op jit(solution)/shard_map/all_to_all | solution.py:165
  89.6 0.7 broadcast_in_dim.12
  90.3 7.6 %all-to-all-start.1 = ((bf16[16,8,896]{2,1,0:T(8,128)(2,1)}), bf16[16,8,896]{2,1,0:T(8,128)(2,1)S(1)}, u32[]{:S(2)}, u32[]{:S(2)}) async-start(bf16[16,8,896]{2,1,0:T(8,128)(2,1)} %broadcast_in_dim.12), calls=%async_computation.1 | async-start | bytes 458752 | tf_op jit(solution)/shard_map/all_to_all | solution.py:104
  97.9 3.0 %collective-permute-start.12 = (bf16[128,896]{1,0:T(8,128)(2,1)S(1)}, bf16[128,896]{1,0:T(8,128)(2,1)S(1)}, u32[]{:S(2)}, u32[]{:S(2)}) collective-permute-start(bf16[128,896]{1,0:T(8,128)(2,1)S(1)} %slice.75), channel_id=1, source_target_pairs={{0,8},{1,9},{2,10},{3,11},{4,12},{5,13},{6,14},{7,15},{8,0},{9,1},... | collective-permute-start | bytes 688136 | tf_op jit(solution)/shard_map/ppermute | solution.py:155
  100.9 6.1 %all-to-all-done.1 = bf16[16,8,896]{2,1,0:T(8,128)(2,1)S(1)} async-done(((bf16[16,8,896]{2,1,0:T(8,128)(2,1)}), bf16[16,8,896]{2,1,0:T(8,128)(2,1)S(1)}, u32[]{:S(2)}, u32[]{:S(2)}) %all-to-all-start.1) | async-done | bytes 229408 | tf_op jit(solution)/shard_map/all_to_all | solution.py:104
  107.0 0.8 broadcast_in_dim.13
  107.8 6.2 %all-to-all-start.2 = ((bf16[16,8,1792]{2,1,0:T(8,128)(2,1)}), bf16[16,8,1792]{2,1,0:T(8,128)(2,1)S(1)}, u32[]{:S(2)}, u32[]{:S(2)}) async-start(bf16[16,8,1792]{2,1,0:T(8,128)(2,1)} %broadcast_in_dim.13), calls=%async_computation.2 | async-start | bytes 917504 | tf_op jit(solution)/shard_map/all_to_all | solution.py:104
  114.0 0.1 broadcast_select_fusion.1
  114.0 0.8 pad_maximum_fusion.1.channel_ref
  114.8 8.3 %all-to-all-done.2 = bf16[16,8,1792]{2,1,0:T(8,128)(2,1)S(1)} async-done(((bf16[16,8,1792]{2,1,0:T(8,128)(2,1)}), bf16[16,8,1792]{2,1,0:T(8,128)(2,1)S(1)}, u32[]{:S(2)}, u32[]{:S(2)}) %all-to-all-start.2) | async-done | bytes 458784 | tf_op jit(solution)/shard_map/all_to_all | solution.py:104
  123.2 0.8 copy-done
  123.9 23.4 %shard_map.64 = bf16[2,201,64,128]{3,2,1,0:T(8,128)(2,1)} custom-call(bf16[128,1792]{1,0:T(8,128)(2,1)} %pad_maximum_fusion.1.channel_ref, bf16[128,1792]{1,0:T(8,128)(2,1)} %bitcast.24), custom_call_target="tpu_custom_call" | custom-call | flops 11802771456 | bytes 8388608 | tf_op jit(solution)/shard_map/pallas_call | solution.py:80
  (25 shorter events, 0.3 us)
Async XLA Ops:
  0.0 26.8 %collective-permute-start.2 = (bf16[128,2048]{1,0:T(8,128)(2,1)}, bf16[128,2048]{1,0:T(8,128)(2,1)S(1)}, u32[]{:S(2)}, u32[]{:S(2)}) collective-permute-start(bf16[128,2048]{1,0:T(8,128)(2,1)} %param.9), channel_id=1, source_target_pairs={{0,8},{1,9},{2,10},{3,11},{4,12},{5,13},{6,14},{7,15},{8,0},{9,1},... | collective-permute-start | bytes 1572872 | tf_op jit(solution)/shard_map/ppermute | solution.py:124
  5.7 14.7 %collective-permute-start.1 = (bf16[128,896]{1,0:T(8,128)(2,1)S(1)}, bf16[128,896]{1,0:T(8,128)(2,1)S(1)}, u32[]{:S(2)}, u32[]{:S(2)}) collective-permute-start(bf16[128,896]{1,0:T(8,128)(2,1)S(1)} %get-tuple-element.24), channel_id=1, source_target_pairs={{0,8},{1,9},{2,10},{3,11},{4,12},{5,13},{6,14},{7,15},{8,0},{9,1},... | collective-permute-start | bytes 688136 | tf_op jit(solution)/shard_map/ppermute | solution.py:123
  6.5 13.2 %collective-permute-start = (s32[2,128]{1,0:T(2,128)S(1)}, s32[2,128]{1,0:T(2,128)S(1)}, u32[]{:S(2)}, u32[]{:S(2)}) collective-permute-start(s32[2,128]{1,0:T(2,128)S(1)} %pad_add_fusion.1), channel_id=1, source_target_pairs={{0,8},{1,9},{2,10},{3,11},{4,12},{5,13},{6,14},{7,15},{8,0},{9,1},... | collective-permute-start | bytes 3080 | tf_op jit(solution)/shard_map/ppermute | solution.py:115
  20.4 18.0 %collective-permute-start.3 = (bf16[256,896]{1,0:T(8,128)(2,1)S(1)}, bf16[256,896]{1,0:T(8,128)(2,1)S(1)}, u32[]{:S(2)}, u32[]{:S(2)}) collective-permute-start(bf16[256,896]{1,0:T(8,128)(2,1)S(1)} %pad_maximum_fusion), channel_id=1, source_target_pairs={{0,1},{1,2},{2,3},{3,4},{4,5},{5,6},{6,7},{7,0},{8,9},{9,10},{10,1... | collective-permute-start | bytes 1376264 | tf_op jit(solution)/shard_map/ppermute | solution.py:140
  22.7 12.2 %collective-permute-start.4 = (bf16[256,896]{1,0:T(8,128)(2,1)S(1)}, bf16[256,896]{1,0:T(8,128)(2,1)S(1)}, u32[]{:S(2)}, u32[]{:S(2)}) collective-permute-start(bf16[256,896]{1,0:T(8,128)(2,1)S(1)} %pad_maximum_fusion), channel_id=1, source_target_pairs={{0,7},{1,0},{2,1},{3,2},{4,3},{5,4},{6,5},{7,6},{8,15},{9,8},{10,9... | collective-permute-start | bytes 1376264 | tf_op jit(solution)/shard_map/ppermute | solution.py:141
  35.0 10.7 %collective-permute-start.6 = (bf16[256,896]{1,0:T(8,128)(2,1)S(1)}, bf16[256,896]{1,0:T(8,128)(2,1)S(1)}, u32[]{:S(2)}, u32[]{:S(2)}) collective-permute-start(bf16[256,896]{1,0:T(8,128)(2,1)S(1)} %collective-permute-done.4), channel_id=1, source_target_pairs={{0,7},{1,0},{2,1},{3,2},{4,3},{5,4},{6,5},{7,6},{8,15},{9,8},{10,9... | collective-permute-start | bytes 1376264 | tf_op jit(solution)/shard_map/ppermute | solution.py:141
  38.4 10.7 %collective-permute-start.5 = (bf16[256,896]{1,0:T(8,128)(2,1)S(1)}, bf16[256,896]{1,0:T(8,128)(2,1)S(1)}, u32[]{:S(2)}, u32[]{:S(2)}) collective-permute-start(bf16[256,896]{1,0:T(8,128)(2,1)S(1)} %collective-permute-done.3), channel_id=1, source_target_pairs={{0,1},{1,2},{2,3},{3,4},{4,5},{5,6},{6,7},{7,0},{8,9},{9,10},{10,1... | collective-permute-start | bytes 1376264 | tf_op jit(solution)/shard_map/ppermute | solution.py:140
  45.7 13.0 %collective-permute-start.8 = (bf16[256,896]{1,0:T(8,128)(2,1)S(1)}, bf16[256,896]{1,0:T(8,128)(2,1)S(1)}, u32[]{:S(2)}, u32[]{:S(2)}) collective-permute-start(bf16[256,896]{1,0:T(8,128)(2,1)S(1)} %collective-permute-done.6), channel_id=1, source_target_pairs={{0,7},{1,0},{2,1},{3,2},{4,3},{5,4},{6,5},{7,6},{8,15},{9,8},{10,9... | collective-permute-start | bytes 1376264 | tf_op jit(solution)/shard_map/ppermute | solution.py:141
  49.1 9.5 %collective-permute-start.7 = (bf16[256,896]{1,0:T(8,128)(2,1)S(1)}, bf16[256,896]{1,0:T(8,128)(2,1)S(1)}, u32[]{:S(2)}, u32[]{:S(2)}) collective-permute-start(bf16[256,896]{1,0:T(8,128)(2,1)S(1)} %collective-permute-done.5), channel_id=1, source_target_pairs={{0,1},{1,2},{2,3},{3,4},{4,5},{5,6},{6,7},{7,0},{8,9},{9,10},{10,1... | collective-permute-start | bytes 1376264 | tf_op jit(solution)/shard_map/ppermute | solution.py:140
  58.6 6.4 %collective-permute-start.9 = (bf16[128,896]{1,0:T(8,128)(2,1)S(1)}, bf16[128,896]{1,0:T(8,128)(2,1)S(1)}, u32[]{:S(2)}, u32[]{:S(2)}) collective-permute-start(bf16[128,896]{1,0:T(8,128)(2,1)S(1)} %slice.72), channel_id=1, source_target_pairs={{0,1},{1,2},{2,3},{3,4},{4,5},{5,6},{6,7},{7,0},{8,9},{9,10},{10,1... | collective-permute-start | bytes 688136 | tf_op jit(solution)/shard_map/ppermute | solution.py:143
  58.8 6.5 %collective-permute-start.10 = (bf16[128,896]{1,0:T(8,128)(2,1)S(1)}, bf16[128,896]{1,0:T(8,128)(2,1)S(1)}, u32[]{:S(2)}, u32[]{:S(2)}) collective-permute-start(bf16[128,896]{1,0:T(8,128)(2,1)S(1)} %slice.73), channel_id=1, source_target_pairs={{0,7},{1,0},{2,1},{3,2},{4,3},{5,4},{6,5},{7,6},{8,15},{9,8},{10,9... | collective-permute-start | bytes 688136 | tf_op jit(solution)/shard_map/ppermute | solution.py:144
  66.3 4.0 %collective-permute-start.11 = (f32[256]{0:T(256)S(1)}, f32[256]{0:T(256)S(1)}, u32[]{:S(2)}, u32[]{:S(2)}) collective-permute-start(f32[256]{0:T(256)S(1)} %get-tuple-element.33), channel_id=1, source_target_pairs={{0,8},{1,9},{2,10},{3,11},{4,12},{5,13},{6,14},{7,15},{8,0},{9,1},... | collective-permute-start | bytes 3080 | tf_op jit(solution)/shard_map/ppermute | solution.py:151
  90.3 16.6 %all-to-all-start.1 = ((bf16[16,8,896]{2,1,0:T(8,128)(2,1)}), bf16[16,8,896]{2,1,0:T(8,128)(2,1)S(1)}, u32[]{:S(2)}, u32[]{:S(2)}) async-start(bf16[16,8,896]{2,1,0:T(8,128)(2,1)} %broadcast_in_dim.12), calls=%async_computation.1 | async-start | bytes 458752 | tf_op jit(solution)/shard_map/all_to_all | solution.py:104
  97.9 16.1 %collective-permute-start.12 = (bf16[128,896]{1,0:T(8,128)(2,1)S(1)}, bf16[128,896]{1,0:T(8,128)(2,1)S(1)}, u32[]{:S(2)}, u32[]{:S(2)}) collective-permute-start(bf16[128,896]{1,0:T(8,128)(2,1)S(1)} %slice.75), channel_id=1, source_target_pairs={{0,8},{1,9},{2,10},{3,11},{4,12},{5,13},{6,14},{7,15},{8,0},{9,1},... | collective-permute-start | bytes 688136 | tf_op jit(solution)/shard_map/ppermute | solution.py:155
  107.8 15.3 %all-to-all-start.2 = ((bf16[16,8,1792]{2,1,0:T(8,128)(2,1)}), bf16[16,8,1792]{2,1,0:T(8,128)(2,1)S(1)}, u32[]{:S(2)}, u32[]{:S(2)}) async-start(bf16[16,8,1792]{2,1,0:T(8,128)(2,1)} %broadcast_in_dim.13), calls=%async_computation.2 | async-start | bytes 917504 | tf_op jit(solution)/shard_map/all_to_all | solution.py:104
  123.2 0.8 copy-start

commit v2 on v0

v2 whole, which is shorter than its diff:
```python
import jax
import jax.numpy as jnp
from jax import lax
from jax.experimental import pallas as pl
from jax.experimental.pallas import tpu as pltpu
from jax.sharding import PartitionSpec as P

SRC = 64
LAG = 100
ROUNDS = 2
LAGS = 201
DEPTH = 8
FINE = 13
COARSE = 8
CHUNK = 2
SPAN = FINE * COARSE

epsilon = 1e-05

CORES = [(s, s ^ 1) for s in range(16)]
ACROSS = [(a * DEPTH + z, (1 - a) * DEPTH + z) for a in range(2) for z in range(DEPTH)]
UP = [(a * DEPTH + z, a * DEPTH + (z + 1) % DEPTH) for a in range(2) for z in range(DEPTH)]
DOWN = [(a * DEPTH + z, a * DEPTH + (z - 1) % DEPTH) for a in range(2) for z in range(DEPTH)]


def correlate_kernel(
    channel_ref, source_ref, out_ref, turned_ref, left_ref, right_ref, stage_ref, sems
):
    rows = source_ref.shape[0]
    channels, samples = channel_ref.shape
    scales = source_ref[:, samples:].astype(jnp.float32)
    scale = (scales[:, :1] + scales[:, 127:]) * (1.0 / float(samples) ** 0.5)
    turned_ref[:SPAN, :] = jnp.zeros((SPAN, channels), jnp.float32)
    turned_ref[SPAN + samples :, :] = jnp.zeros((SPAN, channels), jnp.float32)
    turned_ref[SPAN : SPAN + samples, :] = channel_ref[...].astype(jnp.float32).T

    def place_sources(side):
        padded = jnp.concatenate(
            [source_ref[:, :samples].astype(jnp.float32), jnp.zeros((rows, 128), jnp.float32)],
            axis=1,
        )
        for fine in range(FINE):
            ahead = fine + (1 if side else 1 - FINE)
            moved = pltpu.roll(padded, (-ahead) % (samples + 128), axis=1) if ahead else padded
            left_ref[side, fine * rows : (fine + 1) * rows, :] = moved[:, :samples].astype(
                jnp.bfloat16
            )

    def place_channels(side):
        for coarse in range(COARSE):
            start = SPAN + FINE * (-coarse if side else coarse)
            right_ref[side, :, coarse * channels : (coarse + 1) * channels] = turned_ref[
                start : start + samples, :
            ].astype(jnp.bfloat16)

    def copies(side, begin, some):
        made = []
        for coarse in range(COARSE):
            at = (coarse if side else COARSE - 1 - coarse) * FINE + begin
            lag = at + (LAG + 1 if side else LAG + 1 - SPAN)
            skip, end = max(0, -lag), min(some, LAGS - lag)
            for r in range(ROUNDS if end > skip else 0):
                made.append(
                    pltpu.make_async_copy(
                        stage_ref.at[side, r, pl.ds(at + skip, end - skip)],
                        out_ref.at[r, pl.ds(lag + skip, end - skip)],
                        sems.at[side, r],
                    )
                )
        return made

    place_sources(0)
    place_channels(0)
    for side in range(2):
        for begin in range(0, FINE, CHUNK):
            some = min(CHUNK, FINE - begin)
            products = jnp.dot(
                left_ref[side, begin * rows : (begin + some) * rows, :],
                right_ref[side],
                preferred_element_type=jnp.float32,
            )
            scaled = (products * jnp.concatenate([scale] * some)).astype(jnp.bfloat16)
            for coarse in range(COARSE):
                for fine in range(begin, begin + some):
                    at = (coarse if side else COARSE - 1 - coarse) * FINE + fine
                    for r in range(ROUNDS):
                        top = (fine - begin) * rows + r * SRC
                        stage_ref[side, r, at] = scaled[
                            top : top + SRC, coarse * channels : (coarse + 1) * channels
                        ]
            for copy in copies(side, begin, some):
                copy.start()
        if side == 0:
            place_sources(1)
            place_channels(1)
    for side in range(2):
        for begin in range(0, FINE, CHUNK):
            for copy in copies(side, begin, min(CHUNK, FINE - begin)):
                copy.wait()


def correlate(whitened, sources):
    channels, samples = whitened.shape
    rows = sources.shape[0]
    return pl.pallas_call(
        correlate_kernel,
        out_shape=jax.ShapeDtypeStruct((ROUNDS, LAGS, SRC, channels), jnp.bfloat16),
        in_specs=[pl.BlockSpec(memory_space=pltpu.VMEM)] * 2,
        out_specs=pl.BlockSpec(memory_space=pl.ANY),
        scratch_shapes=[
            pltpu.VMEM((samples + 2 * SPAN, channels), jnp.float32),
            pltpu.VMEM((2, FINE * rows, samples), jnp.bfloat16),
            pltpu.VMEM((2, samples, COARSE * channels), jnp.bfloat16),
            pltpu.VMEM((2, ROUNDS, SPAN, SRC, channels), jnp.bfloat16),
            pltpu.SemaphoreType.DMA((2, ROUNDS)),
        ],
        compiler_params=pltpu.CompilerParams(vmem_limit_bytes=56 * 2**20),
        cost_estimate=pl.CostEstimate(
            flops=2 * LAGS * rows * channels * samples, bytes_accessed=8 * 2**20, transcendentals=0
        ),
    )(whitened, sources)


def everyone(block, axis):
    copies = lax.axis_size(axis)
    tiled = jnp.broadcast_to(block[None], (copies,) + block.shape)
    return lax.all_to_all(tiled, axis, 0, 0)


def on_device(strain, counts, working, mixing, owners, offsets):
    channels, samples = strain.shape
    part = samples // 2
    seg = lax.axis_index("seg")
    grp = lax.axis_index("grp")
    side, level = grp // DEPTH, grp % DEPTH

    core = seg % 2
    fetched = lax.dynamic_slice_in_dim(mixing, core * (channels // 2), channels // 2, 0)
    fetched = lax.ppermute(fetched, "grp", ACROSS)
    valid = jnp.where(working > 0, counts, 0)
    positions = lax.broadcasted_iota(jnp.int32, strain.shape, 1)
    masked = jnp.where(positions < valid[:, None], strain, jnp.zeros_like(strain))
    first, second = masked[:, :part], masked[:, part:]
    mine = jnp.where(side == 0, first, second)

    lanes = lax.broadcasted_iota(jnp.int32, (channels, 128), 1)
    digits = jnp.where(lanes < 64, valid[:, None] >> 7, valid[:, None] & 127)
    theirs = jnp.where(side == 0, second, first)
    theirs = jnp.concatenate([theirs, digits.astype(theirs.dtype)], axis=1)
    theirs = lax.ppermute(theirs, "grp", ACROSS)
    partner = theirs[:, :part]
    high = theirs[:, part].astype(jnp.float32)
    low = theirs[:, part + 127].astype(jnp.float32)
    valid2 = jnp.concatenate([valid, (high * 128.0 + low).astype(jnp.int32)])

    def term(away, who, rows):
        at = (jnp.where(who == 0, side, 1 - side) * DEPTH + (level + away) % DEPTH) * channels
        left = lax.dynamic_slice_in_dim(mixing2, at, channels, 1)
        return jnp.dot(left, rows, preferred_element_type=jnp.float32)

    held = [(0, 0, mine), (0, 1, partner)]
    up, down = [mine, partner], [mine, partner]
    for hop in range(1, DEPTH // 2):
        for who in range(2):
            one = lax.ppermute(up[who], "grp", UP)
            two = lax.ppermute(down[who], "grp", DOWN)
            up[who], down[who] = lax.optimization_barrier((one, two))
            if hop == 1 and who == 1:
                up[who], fetched = lax.optimization_barrier((up[who], fetched))
                handed = lax.ppermute(fetched, "seg", CORES)
            if hop == 2 and who == 1:
                up[who], handed = lax.optimization_barrier((up[who], handed))
            held += [(-hop, who, up[who]), (hop, who, down[who])]
    mixing2 = jnp.concatenate(
        [mixing, jnp.where(core == 0, fetched, handed), jnp.where(core == 0, handed, fetched)]
    )
    held.append((DEPTH // 2, 0, lax.ppermute(up[0], "grp", UP)))
    held.append((DEPTH // 2, 1, lax.ppermute(down[1], "grp", DOWN)))
    coupled = term(*held[0])
    for item in held[1:]:
        coupled = coupled + term(*item)
    block = jnp.concatenate([mine, partner])

    places = side * part + lax.broadcasted_iota(jnp.int32, block.shape, 1)
    usable2 = places < valid2[:, None]
    filtered = jnp.where(usable2, block.astype(jnp.float32) - coupled, jnp.float32(0.0))

    segs = lax.axis_size("seg")
    share = ROUNDS * SRC // segs
    lanes = lax.broadcasted_iota(jnp.int32, (2 * channels, 128), 1)
    digits = jnp.where(lanes < 64, valid2[:, None] >> 7, valid2[:, None] & 127)
    marked = jnp.concatenate(
        [filtered.astype(jnp.bfloat16), digits.astype(jnp.bfloat16)], axis=1
    )
    owner = jnp.repeat(owners, SRC)[:, None]
    place = jnp.repeat(offsets, SRC)[:, None] + jnp.tile(jnp.arange(SRC), ROUNDS)[:, None]
    owner_seg, owner_grp = owner // 16, owner % 16
    place = jnp.where(owner_grp // DEPTH == side, place, place + channels)
    here = (owner_seg == seg) & (owner_grp % DEPTH == level)
    every = lax.broadcasted_iota(jnp.int32, (ROUNDS * SRC, 2 * channels), 1)
    chosen = ((every == place) & here).astype(jnp.bfloat16)
    picked = jnp.dot(chosen, marked, preferred_element_type=jnp.float32).astype(jnp.bfloat16)
    picked = picked.reshape(segs, share, part + 128)
    spread_rows = jnp.sum(lax.all_to_all(picked, "seg", 0, 0), axis=0)
    sums = jnp.sum(filtered * filtered, axis=1, keepdims=True)
    lacking = jnp.broadcast_to(sums[channels:], (channels, 128))
    lacking = jnp.concatenate([filtered[channels:], lacking], axis=1)
    spread_rows, lacking = lax.optimization_barrier((spread_rows, lacking))
    spread_rows = everyone(spread_rows, "grp").reshape(2, DEPTH, share, part + 128)
    spread_rows = jnp.sum(spread_rows, axis=1)
    source = jnp.concatenate([spread_rows[0, :, :part], spread_rows[1, :, :part]], axis=1)
    high = spread_rows[0, :, part : part + 1].astype(jnp.float32)
    low = spread_rows[0, :, part + 127 :].astype(jnp.float32)
    powers = jnp.sum(jnp.square(source.astype(jnp.float32)), axis=1, keepdims=True)
    scale = lax.rsqrt(powers / jnp.maximum(high * 128.0 + low, 1.0) + epsilon)
    coarse = scale.astype(jnp.bfloat16)
    finer = (scale - coarse.astype(jnp.float32)).astype(jnp.bfloat16)
    lanes = lax.broadcasted_iota(jnp.int32, (share, 128), 1)
    scales = jnp.where(lanes < 64, coarse, finer)
    sources = everyone(jnp.concatenate([source, scales], axis=1), "seg")
    sources = sources.reshape(ROUNDS * SRC, samples + 128)

    lacking = lax.ppermute(lacking, "grp", ACROSS)
    sums = sums[:channels] + lacking[:, part : part + 1]
    spread = jnp.sqrt(sums / jnp.maximum(valid, 1).astype(jnp.float32)[:, None] + epsilon)
    kept = (filtered[:channels] / spread).astype(jnp.bfloat16)
    returned = (lacking[:, :part] / spread).astype(jnp.bfloat16)
    whitened = jnp.concatenate(
        [jnp.where(side == 0, kept, returned), jnp.where(side == 0, returned, kept)], axis=1
    )
    return correlate(whitened, sources)


def solution(mesh):
    in_specs = (
        P(("seg", "grp"), None),
        P(("seg", "grp")),
        P(("seg", "grp")),
        P("grp", None),
        P(),
        P(),
    )
    out_specs = P(None, None, None, ("seg", "grp"))
    return jax.shard_map(
        on_device, mesh=mesh, in_specs=in_specs, out_specs=out_specs, check_vma=False
    )
```

time: 628 us -> 126 us (0.20)
  waiting for transfers between devices: 385 us -> 38.9 us
  local copies, waits for them, and re-layouts: 105 us -> 3.67 us
  matrix products: 72.9 us -> 6.08 us
  starting transfers between devices: 0.04 us -> 56.1 us
  loops' own time: 36.5 us -> 0 us
  between operations: 18.4 us -> 0.58 us
  Pallas kernels: 0 us -> 15.5 us
    psum x1 -> x0, waiting for transfers between devices: 249 us -> none  [broadcast(): return lax.psum(kept, axis)]
    all_gather x1 -> x0, waiting for transfers between devices: 136 us -> none  [on_device(): lax.all_gather(masked, 'grp', axis=0, tiled=True)]
    dot_general x53 -> x17, matrix products: 72.9 us -> 6.08 us  [the longest x16 5.1 us: term(): return jnp.dot(left, rows, preferred_element_type=jnp.float32)]
    while x365 -> x0, local copies, waits for them, and re-layouts: 50.1 us -> none
    another operation x2 -> x0, loops' own time: 36.5 us -> none  [correlate(): lax.scan(group_step, jnp.zeros((), jnp.float32), jnp.arange(lag_groups, d...]
    dynamic_slice x53 -> x1, local copies, waits for them, and re-layouts: 31.9 us -> 0.02 us  [on_device(): lax.dynamic_slice_in_dim(mixing, core * (channels // 2), channels // 2, 0)]
    ppermute x0 -> x18, starting transfers between devices: none -> 31.1 us  [the longest x6 15.9 us: on_device(): two = lax.ppermute(down[who], 'grp', DOWN)]
    all_to_all x0 -> x3, starting transfers between devices: none -> 25 us  [the longest x2 13.9 us: everyone(): return lax.all_to_all(tiled, axis, 0, 0)]
  transfers between devices with their start and end apart: 2 -> 21, of which waited for: 2 -> 11; matrix products, arithmetic and copies ran while one was open for 0% -> 6% of each run, Pallas kernels for 0% -> 0%
where the time goes in v2:
time: 126 us
  starting transfers between devices  56.1 us (45%)
  waiting for transfers between devices  38.9 us (31%)
  Pallas kernels  15.5 us (12%)
  matrix products  6.08 us (5%)
  other arithmetic  4.89 us (4%)
  local copies, waits for them, and re-layouts  3.67 us (3%)
    ppermute x6, starting transfers between devices, on_device(): two = lax.ppermute(down[who], 'grp', DOWN)  15.9 us
    pallas_call x1, Pallas kernels, correlate(): pl.pallas_call(correlate_kernel, out_shape=jax.ShapeDtypeStruct((ROUNDS,...  15.5 us
    all_to_all x2, waiting for transfers between devices, everyone(): return lax.all_to_all(tiled, axis, 0, 0)  14.6 us
    all_to_all x2, starting transfers between devices, everyone(): return lax.all_to_all(tiled, axis, 0, 0)  13.9 us
    ppermute x6, waiting for transfers between devices, on_device(): one = lax.ppermute(up[who], 'grp', UP)  11.6 us
    all_to_all x1, starting transfers between devices, on_device(): spread_rows = jnp.sum(lax.all_to_all(picked, 'seg', 0, 0), axis=0)  11.1 us
    all_to_all x1, waiting for transfers between devices, on_device(): spread_rows = jnp.sum(lax.all_to_all(picked, 'seg', 0, 0), axis=0)  7.03 us
    ppermute x1, starting transfers between devices, on_device(): handed = lax.ppermute(fetched, 'seg', CORES)  5.66 us
  transfers between devices with their start and end apart: 21, of which 11 were waited for; matrix products, arithmetic and copies ran while one was open for 6% of the time, Pallas kernels for 0%

profile of v2, /device:TPU:1, one launch (start us, length us, event | category | flops | bytes accessed | tf_op | source)
XLA Modules:
  0.0 125.7 jit_solution(3018033556226942700)
XLA Ops:
  0.0 0.8 broadcast_in_dim.95
  0.9 0.7 iota_add_fusion.1
  1.7 0.7 broadcast_shift-right-arithmetic_fusion.1
  2.4 1.2 fusion.14
  3.7 2.5 %collective-permute-start.7 = (bf16[128,896]{1,0:T(8,128)(2,1)S(1)}, bf16[128,896]{1,0:T(8,128)(2,1)S(1)}, u32[]{:S(2)}, u32[]{:S(2)}) collective-permute-start(bf16[128,896]{1,0:T(8,128)(2,1)S(1)} %get-tuple-element.51), channel_id=1, source_target_pairs={{0,1},{1,2},{2,3},{3,4},{4,5},{5,6},{6,7},{7,0},{8,9},{9,10},{10,1... | collective-permute-start | bytes 688136 | tf_op jit(solution)/shard_map/ppermute | solution.py:165
  6.2 4.0 %collective-permute-start.8 = (bf16[128,896]{1,0:T(8,128)(2,1)S(1)}, bf16[128,896]{1,0:T(8,128)(2,1)S(1)}, u32[]{:S(2)}, u32[]{:S(2)}) collective-permute-start(bf16[128,896]{1,0:T(8,128)(2,1)S(1)} %get-tuple-element.51), channel_id=1, source_target_pairs={{0,7},{1,0},{2,1},{3,2},{4,3},{5,4},{6,5},{7,6},{8,15},{9,8},{10,9... | collective-permute-start | bytes 688136 | tf_op jit(solution)/shard_map/ppermute | solution.py:166
  10.4 2.8 %collective-permute-start = (bf16[128,1024]{1,0:T(8,128)(2,1)S(1)}, bf16[128,1024]{1,0:T(8,128)(2,1)S(1)}, u32[]{:S(2)}, u32[]{:S(2)}) collective-permute-start(bf16[128,1024]{1,0:T(8,128)(2,1)S(1)} %pad_maximum_fusion.3), channel_id=1, source_target_pairs={{0,8},{1,9},{2,10},{3,11},{4,12},{5,13},{6,14},{7,15},{8,0},{9,1},... | collective-permute-start | bytes 786440 | tf_op jit(solution)/shard_map/ppermute | solution.py:150
  13.2 0.3 collective-permute-start.3
  13.7 1.7 %collective-permute-done.7 = bf16[128,896]{1,0:T(8,128)(2,1)S(1)} collective-permute-done((bf16[128,896]{1,0:T(8,128)(2,1)S(1)}, bf16[128,896]{1,0:T(8,128)(2,1)S(1)}, u32[]{:S(2)}, u32[]{:S(2)}) %collective-permute-start.7) | collective-permute-done | bytes 229408 | tf_op jit(solution)/shard_map/ppermute | solution.py:165
  15.5 2.4 %collective-permute-start.10 = (bf16[128,896]{1,0:T(8,128)(2,1)S(1)}, bf16[128,896]{1,0:T(8,128)(2,1)S(1)}, u32[]{:S(2)}, u32[]{:S(2)}) collective-permute-start(bf16[128,896]{1,0:T(8,128)(2,1)S(1)} %collective-permute-done.8), channel_id=1, source_target_pairs={{0,7},{1,0},{2,1},{3,2},{4,3},{5,4},{6,5},{7,6},{8,15},{9,8},{10,9... | collective-permute-start | bytes 688136 | tf_op jit(solution)/shard_map/ppermute | solution.py:166
  17.9 0.9 collective-permute-done
  18.9 2.7 %collective-permute-start.2 = (bf16[128,896]{1,0:T(8,128)(2,1)S(1)}, bf16[128,896]{1,0:T(8,128)(2,1)S(1)}, u32[]{:S(2)}, u32[]{:S(2)}) collective-permute-start(bf16[128,896]{1,0:T(8,128)(2,1)S(1)} %slice.69), channel_id=1, source_target_pairs={{0,7},{1,0},{2,1},{3,2},{4,3},{5,4},{6,5},{7,6},{8,15},{9,8},{10,9... | collective-permute-start | bytes 688136 | tf_op jit(solution)/shard_map/ppermute | solution.py:166
  21.8 2.6 %collective-permute-done.9 = bf16[128,896]{1,0:T(8,128)(2,1)S(1)} collective-permute-done((bf16[128,896]{1,0:T(8,128)(2,1)S(1)}, bf16[128,896]{1,0:T(8,128)(2,1)S(1)}, u32[]{:S(2)}, u32[]{:S(2)}) %collective-permute-start.9) | collective-permute-done | bytes 229408 | tf_op jit(solution)/shard_map/ppermute | solution.py:165
  24.4 2.7 %collective-permute-start.12 = (bf16[128,896]{1,0:T(8,128)(2,1)S(1)}, bf16[128,896]{1,0:T(8,128)(2,1)S(1)}, u32[]{:S(2)}, u32[]{:S(2)}) collective-permute-start(bf16[128,896]{1,0:T(8,128)(2,1)S(1)} %collective-permute-done.10), channel_id=1, source_target_pairs={{0,7},{1,0},{2,1},{3,2},{4,3},{5,4},{6,5},{7,6},{8,15},{9,8},{10,9... | collective-permute-start | bytes 688136 | tf_op jit(solution)/shard_map/ppermute | solution.py:166
  27.1 2.2 %collective-permute-done.1 = bf16[128,896]{1,0:T(8,128)(2,1)S(1)} collective-permute-done((bf16[128,896]{1,0:T(8,128)(2,1)S(1)}, bf16[128,896]{1,0:T(8,128)(2,1)S(1)}, u32[]{:S(2)}, u32[]{:S(2)}) %collective-permute-start.1) | collective-permute-done | bytes 229408 | tf_op jit(solution)/shard_map/ppermute | solution.py:165
  29.3 2.7 %collective-permute-start.5 = (bf16[128,896]{1,0:T(8,128)(2,1)S(1)}, bf16[128,896]{1,0:T(8,128)(2,1)S(1)}, u32[]{:S(2)}, u32[]{:S(2)}) collective-permute-start(bf16[128,896]{1,0:T(8,128)(2,1)S(1)} %collective-permute-done.2), channel_id=1, source_target_pairs={{0,7},{1,0},{2,1},{3,2},{4,3},{5,4},{6,5},{7,6},{8,15},{9,8},{10,9... | collective-permute-start | bytes 688136 | tf_op jit(solution)/shard_map/ppermute | solution.py:166
  32.0 5.7 %collective-permute-start.6 = (bf16[64,2048]{1,0:T(8,128)(2,1)S(1)}, bf16[64,2048]{1,0:T(8,128)(2,1)S(1)}, u32[]{:S(2)}, u32[]{:S(2)}) collective-permute-start(bf16[64,2048]{1,0:T(8,128)(2,1)S(1)} %collective-permute-done.3), channel_id=1, source_target_pairs={{0,16},{16,0},{32,48},{48,32},{64,80},{80,64},{96,112},{112,96},{1... | collective-permute-start | bytes 786440 | tf_op jit(solution)/shard_map/ppermute | solution.py:170
  37.9 1.2 collective-permute-done.4
  39.1 1.4 %collective-permute-start.14 = (bf16[128,896]{1,0:T(8,128)(2,1)S(1)}, bf16[128,896]{1,0:T(8,128)(2,1)S(1)}, u32[]{:S(2)}, u32[]{:S(2)}) collective-permute-start(bf16[128,896]{1,0:T(8,128)(2,1)S(1)} %collective-permute-done.5), channel_id=1, source_target_pairs={{0,7},{1,0},{2,1},{3,2},{4,3},{5,4},{6,5},{7,6},{8,15},{9,8},{10,9... | collective-permute-start | bytes 688136 | tf_op jit(solution)/shard_map/ppermute | solution.py:166
  40.7 0.3 fusion.56
  41.0 0.3 fusion.42
  41.5 0.3 fusion.36
  42.2 0.3 fusion.38
  42.4 0.3 fusion.48
  42.7 0.3 fusion.50
  43.0 0.3 fusion.46
  43.2 0.3 convolution_add_fusion.1
  43.5 0.3 fusion.34
  43.8 1.0 collective-permute-done.15
  45.1 3.8 %collective-permute-done.13 = bf16[128,896]{1,0:T(8,128)(2,1)S(1)} collective-permute-done((bf16[128,896]{1,0:T(8,128)(2,1)S(1)}, bf16[128,896]{1,0:T(8,128)(2,1)S(1)}, u32[]{:S(2)}, u32[]{:S(2)}) %collective-permute-start.13) | collective-permute-done | bytes 229408 | tf_op jit(solution)/shard_map/ppermute | solution.py:165
  48.9 0.6 collective-permute-start.16
  49.8 0.3 fusion.32
  50.0 3.7 %collective-permute-done.16 = bf16[128,896]{1,0:T(8,128)(2,1)S(1)} collective-permute-done((bf16[128,896]{1,0:T(8,128)(2,1)S(1)}, bf16[128,896]{1,0:T(8,128)(2,1)S(1)}, u32[]{:S(2)}, u32[]{:S(2)}) %collective-permute-start.16) | collective-permute-done | bytes 229408 | tf_op jit(solution)/shard_map/ppermute | solution.py:178
  53.8 0.3 fusion.26
  54.0 1.1 fusion.79
  55.2 1.0 fusion.13
  56.1 11.1 %all-to-all-start = ((bf16[16,8,1024]{2,1,0:T(8,128)(2,1)}), bf16[16,8,1024]{2,1,0:T(8,128)(2,1)S(1)}, u32[]{:S(2)}, u32[]{:S(2)}) async-start(bf16[16,8,1024]{2,1,0:T(8,128)(2,1)} %fusion.13), calls=%async_computation | async-start | bytes 524288 | tf_op jit(solution)/shard_map/all_to_all | solution.py:204
  67.3 7.0 %all-to-all-done = bf16[16,8,1024]{2,1,0:T(8,128)(2,1)S(1)} async-done(((bf16[16,8,1024]{2,1,0:T(8,128)(2,1)}), bf16[16,8,1024]{2,1,0:T(8,128)(2,1)S(1)}, u32[]{:S(2)}, u32[]{:S(2)}) %all-to-all-start) | async-done | bytes 262176 | tf_op jit(solution)/shard_map/all_to_all | solution.py:204
  74.4 0.7 broadcast_in_dim.101
  75.1 7.5 %all-to-all-start.1 = ((bf16[16,8,1024]{2,1,0:T(8,128)(2,1)}), bf16[16,8,1024]{2,1,0:T(8,128)(2,1)S(1)}, u32[]{:S(2)}, u32[]{:S(2)}) async-start(bf16[16,8,1024]{2,1,0:T(8,128)(2,1)} %broadcast_in_dim.101), calls=%async_computation.1 | async-start | bytes 524288 | tf_op jit(solution)/shard_map/all_to_all | solution.py:127
  82.9 3.0 %collective-permute-start.17 = (f32[128,1024]{1,0:T(8,128)S(1)}, f32[128,1024]{1,0:T(8,128)S(1)}, u32[]{:S(2)}, u32[]{:S(2)}) collective-permute-start(f32[128,1024]{1,0:T(8,128)S(1)} %pad_maximum_fusion.1), channel_id=1, source_target_pairs={{0,8},{1,9},{2,10},{3,11},{4,12},{5,13},{6,14},{7,15},{8,0},{9,1},... | collective-permute-start | bytes 1572872 | tf_op jit(solution)/shard_map/ppermute | solution.py:223
  85.8 6.2 %all-to-all-done.1 = bf16[16,8,1024]{2,1,0:T(8,128)(2,1)S(1)} async-done(((bf16[16,8,1024]{2,1,0:T(8,128)(2,1)}), bf16[16,8,1024]{2,1,0:T(8,128)(2,1)S(1)}, u32[]{:S(2)}, u32[]{:S(2)}) %all-to-all-start.1) | async-done | bytes 262176 | tf_op jit(solution)/shard_map/all_to_all | solution.py:127
  92.4 0.8 broadcast_in_dim.104
  93.3 6.5 %all-to-all-start.2 = ((bf16[16,8,1920]{2,1,0:T(8,128)(2,1)}), bf16[16,8,1920]{2,1,0:T(8,128)(2,1)S(1)}, u32[]{:S(2)}, u32[]{:S(2)}) async-start(bf16[16,8,1920]{2,1,0:T(8,128)(2,1)} %broadcast_in_dim.104), calls=%async_computation.2 | async-start | bytes 983040 | tf_op jit(solution)/shard_map/all_to_all | solution.py:127
  100.1 0.8 pad_maximum_fusion.2.channel_ref
  100.8 8.4 %all-to-all-done.2 = bf16[16,8,1920]{2,1,0:T(8,128)(2,1)S(1)} async-done(((bf16[16,8,1920]{2,1,0:T(8,128)(2,1)}), bf16[16,8,1920]{2,1,0:T(8,128)(2,1)S(1)}, u32[]{:S(2)}, u32[]{:S(2)}) %all-to-all-start.2) | async-done | bytes 491552 | tf_op jit(solution)/shard_map/all_to_all | solution.py:127
  109.3 0.8 copy-done.1
  110.1 15.5 %shard_map.64 = bf16[2,201,64,128]{3,2,1,0:T(8,128)(2,1)} custom-call(bf16[128,1792]{1,0:T(8,128)(2,1)} %pad_maximum_fusion.2.channel_ref, bf16[128,1920]{1,0:T(8,128)(2,1)} %bitcast.28), custom_call_target="tpu_custom_call" | custom-call | flops 11802771456 | bytes 8388608 | tf_op jit(solution)/shard_map/pallas_call | solution.py:105
  (56 shorter events, 3.4 us)
Async XLA Ops:
  0.0 13.2 %copy-start = (bf16[128,2048]{1,0:T(8,128)(2,1)S(1)}, bf16[128,2048]{1,0:T(8,128)(2,1)}, u32[]{:S(2)}) copy-start(bf16[128,2048]{1,0:T(8,128)(2,1)} %param.9) | copy-start | bytes 1572868
  3.7 11.8 %collective-permute-start.7 = (bf16[128,896]{1,0:T(8,128)(2,1)S(1)}, bf16[128,896]{1,0:T(8,128)(2,1)S(1)}, u32[]{:S(2)}, u32[]{:S(2)}) collective-permute-start(bf16[128,896]{1,0:T(8,128)(2,1)S(1)} %get-tuple-element.51), channel_id=1, source_target_pairs={{0,1},{1,2},{2,3},{3,4},{4,5},{5,6},{6,7},{7,0},{8,9},{9,10},{10,1... | collective-permute-start | bytes 688136 | tf_op jit(solution)/shard_map/ppermute | solution.py:165
  6.2 9.3 %collective-permute-start.8 = (bf16[128,896]{1,0:T(8,128)(2,1)S(1)}, bf16[128,896]{1,0:T(8,128)(2,1)S(1)}, u32[]{:S(2)}, u32[]{:S(2)}) collective-permute-start(bf16[128,896]{1,0:T(8,128)(2,1)S(1)} %get-tuple-element.51), channel_id=1, source_target_pairs={{0,7},{1,0},{2,1},{3,2},{4,3},{5,4},{6,5},{7,6},{8,15},{9,8},{10,9... | collective-permute-start | bytes 688136 | tf_op jit(solution)/shard_map/ppermute | solution.py:166
  10.4 8.4 %collective-permute-start = (bf16[128,1024]{1,0:T(8,128)(2,1)S(1)}, bf16[128,1024]{1,0:T(8,128)(2,1)S(1)}, u32[]{:S(2)}, u32[]{:S(2)}) collective-permute-start(bf16[128,1024]{1,0:T(8,128)(2,1)S(1)} %pad_maximum_fusion.3), channel_id=1, source_target_pairs={{0,8},{1,9},{2,10},{3,11},{4,12},{5,13},{6,14},{7,15},{8,0},{9,1},... | collective-permute-start | bytes 786440 | tf_op jit(solution)/shard_map/ppermute | solution.py:150
  13.2 16.1 %collective-permute-start.3 = (bf16[64,2048]{1,0:T(8,128)(2,1)S(1)}, bf16[64,2048]{1,0:T(8,128)(2,1)S(1)}, u32[]{:S(2)}, u32[]{:S(2)}) collective-permute-start(bf16[64,2048]{1,0:T(8,128)(2,1)S(1)} %constant_dynamic-slice_fusion), channel_id=1, source_target_pairs={{0,8},{1,9},{2,10},{3,11},{4,12},{5,13},{6,14},{7,15},{8,0},{9,1},... | collective-permute-start | bytes 786440 | tf_op jit(solution)/shard_map/ppermute | solution.py:139
  15.5 6.3 %collective-permute-start.10 = (bf16[128,896]{1,0:T(8,128)(2,1)S(1)}, bf16[128,896]{1,0:T(8,128)(2,1)S(1)}, u32[]{:S(2)}, u32[]{:S(2)}) collective-permute-start(bf16[128,896]{1,0:T(8,128)(2,1)S(1)} %collective-permute-done.8), channel_id=1, source_target_pairs={{0,7},{1,0},{2,1},{3,2},{4,3},{5,4},{6,5},{7,6},{8,15},{9,8},{10,9... | collective-permute-start | bytes 688136 | tf_op jit(solution)/shard_map/ppermute | solution.py:166
  17.9 6.5 %collective-permute-start.9 = (bf16[128,896]{1,0:T(8,128)(2,1)S(1)}, bf16[128,896]{1,0:T(8,128)(2,1)S(1)}, u32[]{:S(2)}, u32[]{:S(2)}) collective-permute-start(bf16[128,896]{1,0:T(8,128)(2,1)S(1)} %collective-permute-done.7), channel_id=1, source_target_pairs={{0,1},{1,2},{2,3},{3,4},{4,5},{5,6},{6,7},{7,0},{8,9},{9,10},{10,1... | collective-permute-start | bytes 688136 | tf_op jit(solution)/shard_map/ppermute | solution.py:165
  18.8 10.5 %collective-permute-start.1 = (bf16[128,896]{1,0:T(8,128)(2,1)S(1)}, bf16[128,896]{1,0:T(8,128)(2,1)S(1)}, u32[]{:S(2)}, u32[]{:S(2)}) collective-permute-start(bf16[128,896]{1,0:T(8,128)(2,1)S(1)} %slice.69), channel_id=1, source_target_pairs={{0,1},{1,2},{2,3},{3,4},{4,5},{5,6},{6,7},{7,0},{8,9},{9,10},{10,1... | collective-permute-start | bytes 688136 | tf_op jit(solution)/shard_map/ppermute | solution.py:165
  18.9 10.4 %collective-permute-start.2 = (bf16[128,896]{1,0:T(8,128)(2,1)S(1)}, bf16[128,896]{1,0:T(8,128)(2,1)S(1)}, u32[]{:S(2)}, u32[]{:S(2)}) collective-permute-start(bf16[128,896]{1,0:T(8,128)(2,1)S(1)} %slice.69), channel_id=1, source_target_pairs={{0,7},{1,0},{2,1},{3,2},{4,3},{5,4},{6,5},{7,6},{8,15},{9,8},{10,9... | collective-permute-start | bytes 688136 | tf_op jit(solution)/shard_map/ppermute | solution.py:166
  24.4 13.4 %collective-permute-start.11 = (bf16[128,896]{1,0:T(8,128)(2,1)S(1)}, bf16[128,896]{1,0:T(8,128)(2,1)S(1)}, u32[]{:S(2)}, u32[]{:S(2)}) collective-permute-start(bf16[128,896]{1,0:T(8,128)(2,1)S(1)} %collective-permute-done.9), channel_id=1, source_target_pairs={{0,1},{1,2},{2,3},{3,4},{4,5},{5,6},{6,7},{7,0},{8,9},{9,10},{10,1... | collective-permute-start | bytes 688136 | tf_op jit(solution)/shard_map/ppermute | solution.py:165
  24.4 13.4 %collective-permute-start.12 = (bf16[128,896]{1,0:T(8,128)(2,1)S(1)}, bf16[128,896]{1,0:T(8,128)(2,1)S(1)}, u32[]{:S(2)}, u32[]{:S(2)}) collective-permute-start(bf16[128,896]{1,0:T(8,128)(2,1)S(1)} %collective-permute-done.10), channel_id=1, source_target_pairs={{0,7},{1,0},{2,1},{3,2},{4,3},{5,4},{6,5},{7,6},{8,15},{9,8},{10,9... | collective-permute-start | bytes 688136 | tf_op jit(solution)/shard_map/ppermute | solution.py:166
  29.3 9.8 %collective-permute-start.4 = (bf16[128,896]{1,0:T(8,128)(2,1)S(1)}, bf16[128,896]{1,0:T(8,128)(2,1)S(1)}, u32[]{:S(2)}, u32[]{:S(2)}) collective-permute-start(bf16[128,896]{1,0:T(8,128)(2,1)S(1)} %collective-permute-done.1), channel_id=1, source_target_pairs={{0,1},{1,2},{2,3},{3,4},{4,5},{5,6},{6,7},{7,0},{8,9},{9,10},{10,1... | collective-permute-start | bytes 688136 | tf_op jit(solution)/shard_map/ppermute | solution.py:165
  29.3 9.8 %collective-permute-start.5 = (bf16[128,896]{1,0:T(8,128)(2,1)S(1)}, bf16[128,896]{1,0:T(8,128)(2,1)S(1)}, u32[]{:S(2)}, u32[]{:S(2)}) collective-permute-start(bf16[128,896]{1,0:T(8,128)(2,1)S(1)} %collective-permute-done.2), channel_id=1, source_target_pairs={{0,7},{1,0},{2,1},{3,2},{4,3},{5,4},{6,5},{7,6},{8,15},{9,8},{10,9... | collective-permute-start | bytes 688136 | tf_op jit(solution)/shard_map/ppermute | solution.py:166
  32.0 8.6 %collective-permute-start.6 = (bf16[64,2048]{1,0:T(8,128)(2,1)S(1)}, bf16[64,2048]{1,0:T(8,128)(2,1)S(1)}, u32[]{:S(2)}, u32[]{:S(2)}) collective-permute-start(bf16[64,2048]{1,0:T(8,128)(2,1)S(1)} %collective-permute-done.3), channel_id=1, source_target_pairs={{0,16},{16,0},{32,48},{48,32},{64,80},{80,64},{96,112},{112,96},{1... | collective-permute-start | bytes 786440 | tf_op jit(solution)/shard_map/ppermute | solution.py:170
  37.8 7.0 %collective-permute-start.15 = (bf16[128,896]{1,0:T(8,128)(2,1)S(1)}, bf16[128,896]{1,0:T(8,128)(2,1)S(1)}, u32[]{:S(2)}, u32[]{:S(2)}) collective-permute-start(bf16[128,896]{1,0:T(8,128)(2,1)S(1)} %collective-permute-done.11), channel_id=1, source_target_pairs={{0,1},{1,2},{2,3},{3,4},{4,5},{5,6},{6,7},{7,0},{8,9},{9,10},{10,1... | collective-permute-start | bytes 688136 | tf_op jit(solution)/shard_map/ppermute | solution.py:177
  39.1 5.9 %collective-permute-start.14 = (bf16[128,896]{1,0:T(8,128)(2,1)S(1)}, bf16[128,896]{1,0:T(8,128)(2,1)S(1)}, u32[]{:S(2)}, u32[]{:S(2)}) collective-permute-start(bf16[128,896]{1,0:T(8,128)(2,1)S(1)} %collective-permute-done.5), channel_id=1, source_target_pairs={{0,7},{1,0},{2,1},{3,2},{4,3},{5,4},{6,5},{7,6},{8,15},{9,8},{10,9... | collective-permute-start | bytes 688136 | tf_op jit(solution)/shard_map/ppermute | solution.py:166
  41.8 7.1 %collective-permute-start.13 = (bf16[128,896]{1,0:T(8,128)(2,1)S(1)}, bf16[128,896]{1,0:T(8,128)(2,1)S(1)}, u32[]{:S(2)}, u32[]{:S(2)}) collective-permute-start(bf16[128,896]{1,0:T(8,128)(2,1)S(1)} %collective-permute-done.4), channel_id=1, source_target_pairs={{0,1},{1,2},{2,3},{3,4},{4,5},{5,6},{6,7},{7,0},{8,9},{9,10},{10,1... | collective-permute-start | bytes 688136 | tf_op jit(solution)/shard_map/ppermute | solution.py:165
  48.9 4.9 %collective-permute-start.16 = (bf16[128,896]{1,0:T(8,128)(2,1)S(1)}, bf16[128,896]{1,0:T(8,128)(2,1)S(1)}, u32[]{:S(2)}, u32[]{:S(2)}) collective-permute-start(bf16[128,896]{1,0:T(8,128)(2,1)S(1)} %collective-permute-done.14), channel_id=1, source_target_pairs={{0,7},{1,0},{2,1},{3,2},{4,3},{5,4},{6,5},{7,6},{8,15},{9,8},{10,9... | collective-permute-start | bytes 688136 | tf_op jit(solution)/shard_map/ppermute | solution.py:178
  56.1 18.2 %all-to-all-start = ((bf16[16,8,1024]{2,1,0:T(8,128)(2,1)}), bf16[16,8,1024]{2,1,0:T(8,128)(2,1)S(1)}, u32[]{:S(2)}, u32[]{:S(2)}) async-start(bf16[16,8,1024]{2,1,0:T(8,128)(2,1)} %fusion.13), calls=%async_computation | async-start | bytes 524288 | tf_op jit(solution)/shard_map/all_to_all | solution.py:204
  75.1 16.8 %all-to-all-start.1 = ((bf16[16,8,1024]{2,1,0:T(8,128)(2,1)}), bf16[16,8,1024]{2,1,0:T(8,128)(2,1)S(1)}, u32[]{:S(2)}, u32[]{:S(2)}) async-start(bf16[16,8,1024]{2,1,0:T(8,128)(2,1)} %broadcast_in_dim.101), calls=%async_computation.1 | async-start | bytes 524288 | tf_op jit(solution)/shard_map/all_to_all | solution.py:127
  82.9 16.9 %collective-permute-start.17 = (f32[128,1024]{1,0:T(8,128)S(1)}, f32[128,1024]{1,0:T(8,128)S(1)}, u32[]{:S(2)}, u32[]{:S(2)}) collective-permute-start(f32[128,1024]{1,0:T(8,128)S(1)} %pad_maximum_fusion.1), channel_id=1, source_target_pairs={{0,8},{1,9},{2,10},{3,11},{4,12},{5,13},{6,14},{7,15},{8,0},{9,1},... | collective-permute-start | bytes 1572872 | tf_op jit(solution)/shard_map/ppermute | solution.py:223
  93.3 16.0 %all-to-all-start.2 = ((bf16[16,8,1920]{2,1,0:T(8,128)(2,1)}), bf16[16,8,1920]{2,1,0:T(8,128)(2,1)S(1)}, u32[]{:S(2)}, u32[]{:S(2)}) async-start(bf16[16,8,1920]{2,1,0:T(8,128)(2,1)} %broadcast_in_dim.104), calls=%async_computation.2 | async-start | bytes 983040 | tf_op jit(solution)/shard_map/all_to_all | solution.py:127
  109.3 0.8 copy-start.1

commit v3 on v2

--- a/solution.py
+++ b/solution.py
@@ -164,11 +164,13 @@
         for who in range(2):
             one = lax.ppermute(up[who], "grp", UP)
             two = lax.ppermute(down[who], "grp", DOWN)
-            up[who], down[who] = lax.optimization_barrier((one, two))
+            if hop < 3 or who == 0:
+                one, two = lax.optimization_barrier((one, two))
+            up[who], down[who] = one, two
             if hop == 1 and who == 1:
                 up[who], fetched = lax.optimization_barrier((up[who], fetched))
                 handed = lax.ppermute(fetched, "seg", CORES)
-            if hop == 2 and who == 1:
+            if hop == 3 and who == 0:
                 up[who], handed = lax.optimization_barrier((up[who], handed))
             held += [(-hop, who, up[who]), (hop, who, down[who])]
     mixing2 = jnp.concatenate(

time: 126 us -> 122 us (0.968)
  waiting for transfers between devices: 38.9 us -> 35.9 us
    ppermute x1, waiting for transfers between devices: 3.72 us -> 0.01 us  [on_device(): held.append((DEPTH // 2, 1, lax.ppermute(down[1], 'grp', DOWN)))]
    all_to_all x1, starting transfers between devices: 11.1 us -> 7.72 us  [on_device(): spread_rows = jnp.sum(lax.all_to_all(picked, 'seg', 0, 0), axis=0)]
    ppermute x1, waiting for transfers between devices: 0.98 us -> 4.09 us  [on_device(): held.append((DEPTH // 2, 0, lax.ppermute(up[0], 'grp', UP)))]
    ppermute x1, starting transfers between devices: 0.61 us -> 3.22 us  [on_device(): held.append((DEPTH // 2, 1, lax.ppermute(down[1], 'grp', DOWN)))]
    ppermute x6, starting transfers between devices: 2.74 us -> 5.07 us  [on_device(): one = lax.ppermute(up[who], 'grp', UP)]
    ppermute x6, waiting for transfers between devices: 11.6 us -> 9.33 us  [on_device(): one = lax.ppermute(up[who], 'grp', UP)]
    ppermute x6, starting transfers between devices: 15.9 us -> 14.6 us  [on_device(): two = lax.ppermute(down[who], 'grp', DOWN)]
  transfers between devices with their start and end apart: 21 -> 21, of which waited for: 11 -> 11; matrix products, arithmetic and copies ran while one was open for 6% -> 7% of each run, Pallas kernels for 0% -> 0%
where the time goes in v3:
time: 122 us
  starting transfers between devices  56.3 us (46%)
  waiting for transfers between devices  35.9 us (29%)
  Pallas kernels  15.5 us (13%)
  matrix products  5.94 us (5%)
  other arithmetic  4.31 us (4%)
  local copies, waits for them, and re-layouts  2.96 us (2%)
    pallas_call x1, Pallas kernels, correlate(): pl.pallas_call(correlate_kernel, out_shape=jax.ShapeDtypeStruct((ROUNDS,...  15.5 us
    ppermute x6, starting transfers between devices, on_device(): two = lax.ppermute(down[who], 'grp', DOWN)  14.6 us
    all_to_all x2, waiting for transfers between devices, everyone(): return lax.all_to_all(tiled, axis, 0, 0)  14.6 us
    all_to_all x2, starting transfers between devices, everyone(): return lax.all_to_all(tiled, axis, 0, 0)  13.7 us
    ppermute x6, waiting for transfers between devices, on_device(): one = lax.ppermute(up[who], 'grp', UP)  9.33 us
    all_to_all x1, starting transfers between devices, on_device(): spread_rows = jnp.sum(lax.all_to_all(picked, 'seg', 0, 0), axis=0)  7.72 us
    all_to_all x1, waiting for transfers between devices, on_device(): spread_rows = jnp.sum(lax.all_to_all(picked, 'seg', 0, 0), axis=0)  6.99 us
    ppermute x1, starting transfers between devices, on_device(): handed = lax.ppermute(fetched, 'seg', CORES)  5.18 us
  transfers between devices with their start and end apart: 21, of which 11 were waited for; matrix products, arithmetic and copies ran while one was open for 7% of the time, Pallas kernels for 0%

profile of v3, /device:TPU:1, one launch (start us, length us, event | category | flops | bytes accessed | tf_op | source)
XLA Modules:
  0.0 121.5 jit_solution(11684344910713058779)
XLA Ops:
  0.0 0.7 broadcast_shift-right-arithmetic_fusion.1
  0.8 1.2 %fusion.15 = bf16[128,1792]{1,0:T(8,128)(2,1)S(1)} fusion(bf16[128,1792]{1,0:T(8,128)(2,1)} %param.6, s32[128]{0:T(128)S(1)} %get-tuple-element.40), kind=kLoop, calls=%fused_computation.22 | loop fusion | flops 458752 | bytes 918016 | tf_op jit(solution)/shard_map/jit(_where)/select_n | solution.py:142
  2.0 2.5 %collective-permute-start.4 = (bf16[128,896]{1,0:T(8,128)(2,1)S(1)}, bf16[128,896]{1,0:T(8,128)(2,1)S(1)}, u32[]{:S(2)}, u32[]{:S(2)}) collective-permute-start(bf16[128,896]{1,0:T(8,128)(2,1)S(1)} %get-tuple-element.48), channel_id=1, source_target_pairs={{0,1},{1,2},{2,3},{3,4},{4,5},{5,6},{6,7},{7,0},{8,9},{9,10},{10,1... | collective-permute-start | bytes 688136 | tf_op jit(solution)/shard_map/ppermute | solution.py:165
  4.6 4.0 %collective-permute-start.5 = (bf16[128,896]{1,0:T(8,128)(2,1)S(1)}, bf16[128,896]{1,0:T(8,128)(2,1)S(1)}, u32[]{:S(2)}, u32[]{:S(2)}) collective-permute-start(bf16[128,896]{1,0:T(8,128)(2,1)S(1)} %get-tuple-element.48), channel_id=1, source_target_pairs={{0,7},{1,0},{2,1},{3,2},{4,3},{5,4},{6,5},{7,6},{8,15},{9,8},{10,9... | collective-permute-start | bytes 688136 | tf_op jit(solution)/shard_map/ppermute | solution.py:166
  8.8 2.8 %collective-permute-start = (bf16[128,1024]{1,0:T(8,128)(2,1)S(1)}, bf16[128,1024]{1,0:T(8,128)(2,1)S(1)}, u32[]{:S(2)}, u32[]{:S(2)}) collective-permute-start(bf16[128,1024]{1,0:T(8,128)(2,1)S(1)} %pad_maximum_fusion.3), channel_id=1, source_target_pairs={{0,8},{1,9},{2,10},{3,11},{4,12},{5,13},{6,14},{7,15},{8,0},{9,1},... | collective-permute-start | bytes 786440 | tf_op jit(solution)/shard_map/ppermute | solution.py:150
  11.6 0.3 collective-permute-start.3
  12.5 1.4 %collective-permute-done.4 = bf16[128,896]{1,0:T(8,128)(2,1)S(1)} collective-permute-done((bf16[128,896]{1,0:T(8,128)(2,1)S(1)}, bf16[128,896]{1,0:T(8,128)(2,1)S(1)}, u32[]{:S(2)}, u32[]{:S(2)}) %collective-permute-start.4) | collective-permute-done | bytes 229408 | tf_op jit(solution)/shard_map/ppermute | solution.py:165
  13.9 2.7 %collective-permute-start.7 = (bf16[128,896]{1,0:T(8,128)(2,1)S(1)}, bf16[128,896]{1,0:T(8,128)(2,1)S(1)}, u32[]{:S(2)}, u32[]{:S(2)}) collective-permute-start(bf16[128,896]{1,0:T(8,128)(2,1)S(1)} %collective-permute-done.5), channel_id=1, source_target_pairs={{0,7},{1,0},{2,1},{3,2},{4,3},{5,4},{6,5},{7,6},{8,15},{9,8},{10,9... | collective-permute-start | bytes 688136 | tf_op jit(solution)/shard_map/ppermute | solution.py:166
  16.5 0.7 collective-permute-done
  17.3 2.7 %collective-permute-start.2 = (bf16[128,896]{1,0:T(8,128)(2,1)S(1)}, bf16[128,896]{1,0:T(8,128)(2,1)S(1)}, u32[]{:S(2)}, u32[]{:S(2)}) collective-permute-start(bf16[128,896]{1,0:T(8,128)(2,1)S(1)} %slice.69), channel_id=1, source_target_pairs={{0,7},{1,0},{2,1},{3,2},{4,3},{5,4},{6,5},{7,6},{8,15},{9,8},{10,9... | collective-permute-start | bytes 688136 | tf_op jit(solution)/shard_map/ppermute | solution.py:166
  20.2 0.8 collective-permute-done.6
  20.9 0.9 collective-permute-start.8
  21.8 1.8 %collective-permute-start.9 = (bf16[128,896]{1,0:T(8,128)(2,1)S(1)}, bf16[128,896]{1,0:T(8,128)(2,1)S(1)}, u32[]{:S(2)}, u32[]{:S(2)}) collective-permute-start(bf16[128,896]{1,0:T(8,128)(2,1)S(1)} %collective-permute-done.7), channel_id=1, source_target_pairs={{0,7},{1,0},{2,1},{3,2},{4,3},{5,4},{6,5},{7,6},{8,15},{9,8},{10,9... | collective-permute-start | bytes 688136 | tf_op jit(solution)/shard_map/ppermute | solution.py:166
  23.6 1.6 %collective-permute-done.1 = bf16[128,896]{1,0:T(8,128)(2,1)S(1)} collective-permute-done((bf16[128,896]{1,0:T(8,128)(2,1)S(1)}, bf16[128,896]{1,0:T(8,128)(2,1)S(1)}, u32[]{:S(2)}, u32[]{:S(2)}) %collective-permute-start.1) | collective-permute-done | bytes 229408 | tf_op jit(solution)/shard_map/ppermute | solution.py:165
  25.2 5.2 %collective-permute-start.10 = (bf16[64,2048]{1,0:T(8,128)(2,1)S(1)}, bf16[64,2048]{1,0:T(8,128)(2,1)S(1)}, u32[]{:S(2)}, u32[]{:S(2)}) collective-permute-start(bf16[64,2048]{1,0:T(8,128)(2,1)S(1)} %collective-permute-done.3), channel_id=1, source_target_pairs={{0,16},{16,0},{32,48},{48,32},{64,80},{80,64},{96,112},{112,96},{1... | collective-permute-start | bytes 786440 | tf_op jit(solution)/shard_map/ppermute | solution.py:172
  30.4 1.5 %collective-permute-start.11 = (bf16[128,896]{1,0:T(8,128)(2,1)S(1)}, bf16[128,896]{1,0:T(8,128)(2,1)S(1)}, u32[]{:S(2)}, u32[]{:S(2)}) collective-permute-start(bf16[128,896]{1,0:T(8,128)(2,1)S(1)} %collective-permute-done.1), channel_id=1, source_target_pairs={{0,1},{1,2},{2,3},{3,4},{4,5},{5,6},{6,7},{7,0},{8,9},{9,10},{10,1... | collective-permute-start | bytes 688136 | tf_op jit(solution)/shard_map/ppermute | solution.py:165
  31.9 1.2 collective-permute-start.12
  33.3 5.6 %collective-permute-done.11 = bf16[128,896]{1,0:T(8,128)(2,1)S(1)} collective-permute-done((bf16[128,896]{1,0:T(8,128)(2,1)S(1)}, bf16[128,896]{1,0:T(8,128)(2,1)S(1)}, u32[]{:S(2)}, u32[]{:S(2)}) %collective-permute-start.11) | collective-permute-done | bytes 229408 | tf_op jit(solution)/shard_map/ppermute | solution.py:165
  39.0 2.3 %collective-permute-start.14 = (bf16[128,896]{1,0:T(8,128)(2,1)S(1)}, bf16[128,896]{1,0:T(8,128)(2,1)S(1)}, u32[]{:S(2)}, u32[]{:S(2)}) collective-permute-start(bf16[128,896]{1,0:T(8,128)(2,1)S(1)} %collective-permute-done.12), channel_id=1, source_target_pairs={{0,7},{1,0},{2,1},{3,2},{4,3},{5,4},{6,5},{7,6},{8,15},{9,8},{10,9... | collective-permute-start | bytes 688136 | tf_op jit(solution)/shard_map/ppermute | solution.py:166
  41.3 0.7 collective-permute-start.15
  42.1 0.3 fusion.36
  42.4 0.3 fusion.38
  42.7 0.3 fusion.40
  43.0 0.3 fusion.42
  43.5 0.3 fusion.46
  43.8 0.3 fusion.48
  44.0 0.3 fusion.50
  44.3 0.3 fusion.54
  44.6 0.3 convolution_add_fusion.2
  44.9 0.3 fusion.34
  45.2 3.2 %collective-permute-start.16 = (bf16[128,896]{1,0:T(8,128)(2,1)S(1)}, bf16[128,896]{1,0:T(8,128)(2,1)S(1)}, u32[]{:S(2)}, u32[]{:S(2)}) collective-permute-start(bf16[128,896]{1,0:T(8,128)(2,1)S(1)} %collective-permute-done.14), channel_id=1, source_target_pairs={{0,7},{1,0},{2,1},{3,2},{4,3},{5,4},{6,5},{7,6},{8,15},{9,8},{10,9... | collective-permute-start | bytes 688136 | tf_op jit(solution)/shard_map/ppermute | solution.py:180
  48.7 0.3 fusion.32
  49.0 4.1 %collective-permute-done.15 = bf16[128,896]{1,0:T(8,128)(2,1)S(1)} collective-permute-done((bf16[128,896]{1,0:T(8,128)(2,1)S(1)}, bf16[128,896]{1,0:T(8,128)(2,1)S(1)}, u32[]{:S(2)}, u32[]{:S(2)}) %collective-permute-start.15) | collective-permute-done | bytes 229408 | tf_op jit(solution)/shard_map/ppermute | solution.py:179
  53.4 0.7 fusion.13
  54.1 0.5 fusion.77
  54.6 1.0 fusion.14
  55.6 7.7 %all-to-all-start = ((bf16[16,8,1024]{2,1,0:T(8,128)(2,1)}), bf16[16,8,1024]{2,1,0:T(8,128)(2,1)S(1)}, u32[]{:S(2)}, u32[]{:S(2)}) async-start(bf16[16,8,1024]{2,1,0:T(8,128)(2,1)} %fusion.14), calls=%async_computation | async-start | bytes 524288 | tf_op jit(solution)/shard_map/all_to_all | solution.py:206
  63.5 7.0 %all-to-all-done = bf16[16,8,1024]{2,1,0:T(8,128)(2,1)S(1)} async-done(((bf16[16,8,1024]{2,1,0:T(8,128)(2,1)}), bf16[16,8,1024]{2,1,0:T(8,128)(2,1)S(1)}, u32[]{:S(2)}, u32[]{:S(2)}) %all-to-all-start) | async-done | bytes 262176 | tf_op jit(solution)/shard_map/all_to_all | solution.py:206
  70.5 0.7 broadcast_in_dim.101
  71.2 7.2 %all-to-all-start.1 = ((bf16[16,8,1024]{2,1,0:T(8,128)(2,1)}), bf16[16,8,1024]{2,1,0:T(8,128)(2,1)S(1)}, u32[]{:S(2)}, u32[]{:S(2)}) async-start(bf16[16,8,1024]{2,1,0:T(8,128)(2,1)} %broadcast_in_dim.101), calls=%async_computation.1 | async-start | bytes 524288 | tf_op jit(solution)/shard_map/all_to_all | solution.py:127
  78.6 3.0 %collective-permute-start.17 = (f32[128,1024]{1,0:T(8,128)S(1)}, f32[128,1024]{1,0:T(8,128)S(1)}, u32[]{:S(2)}, u32[]{:S(2)}) collective-permute-start(f32[128,1024]{1,0:T(8,128)S(1)} %pad_maximum_fusion.1), channel_id=1, source_target_pairs={{0,8},{1,9},{2,10},{3,11},{4,12},{5,13},{6,14},{7,15},{8,0},{9,1},... | collective-permute-start | bytes 1572872 | tf_op jit(solution)/shard_map/ppermute | solution.py:225
  81.6 6.2 %all-to-all-done.1 = bf16[16,8,1024]{2,1,0:T(8,128)(2,1)S(1)} async-done(((bf16[16,8,1024]{2,1,0:T(8,128)(2,1)}), bf16[16,8,1024]{2,1,0:T(8,128)(2,1)S(1)}, u32[]{:S(2)}, u32[]{:S(2)}) %all-to-all-start.1) | async-done | bytes 262176 | tf_op jit(solution)/shard_map/all_to_all | solution.py:127
  88.2 0.8 broadcast_in_dim.104
  89.1 6.5 %all-to-all-start.2 = ((bf16[16,8,1920]{2,1,0:T(8,128)(2,1)}), bf16[16,8,1920]{2,1,0:T(8,128)(2,1)S(1)}, u32[]{:S(2)}, u32[]{:S(2)}) async-start(bf16[16,8,1920]{2,1,0:T(8,128)(2,1)} %broadcast_in_dim.104), calls=%async_computation.2 | async-start | bytes 983040 | tf_op jit(solution)/shard_map/all_to_all | solution.py:127
  95.8 0.8 pad_maximum_fusion.2.channel_ref
  96.6 8.4 %all-to-all-done.2 = bf16[16,8,1920]{2,1,0:T(8,128)(2,1)S(1)} async-done(((bf16[16,8,1920]{2,1,0:T(8,128)(2,1)}), bf16[16,8,1920]{2,1,0:T(8,128)(2,1)S(1)}, u32[]{:S(2)}, u32[]{:S(2)}) %all-to-all-start.2) | async-done | bytes 491552 | tf_op jit(solution)/shard_map/all_to_all | solution.py:127
  105.1 0.8 copy-done.1
  105.8 15.5 %shard_map.64 = bf16[2,201,64,128]{3,2,1,0:T(8,128)(2,1)} custom-call(bf16[128,1792]{1,0:T(8,128)(2,1)} %pad_maximum_fusion.2.channel_ref, bf16[128,1920]{1,0:T(8,128)(2,1)} %bitcast.28), custom_call_target="tpu_custom_call" | custom-call | flops 11802771456 | bytes 8388608 | tf_op jit(solution)/shard_map/pallas_call | solution.py:105
  (61 shorter events, 3.3 us)
Async XLA Ops:
  0.0 11.6 %copy-start = (bf16[128,2048]{1,0:T(8,128)(2,1)S(1)}, bf16[128,2048]{1,0:T(8,128)(2,1)}, u32[]{:S(2)}) copy-start(bf16[128,2048]{1,0:T(8,128)(2,1)} %param.9) | copy-start | bytes 1572868
  0.0 11.9 %copy-start.2 = (s32[2]{0:T(128)S(1)}, s32[2]{0:T(128)}, u32[]{:S(2)}) copy-start(s32[2]{0:T(128)} %param.11) | copy-start | bytes 28
  0.0 12.1 %copy-start.3 = (s32[2]{0:T(128)S(1)}, s32[2]{0:T(128)}, u32[]{:S(2)}) copy-start(s32[2]{0:T(128)} %param.10) | copy-start | bytes 28
  2.0 11.8 %collective-permute-start.4 = (bf16[128,896]{1,0:T(8,128)(2,1)S(1)}, bf16[128,896]{1,0:T(8,128)(2,1)S(1)}, u32[]{:S(2)}, u32[]{:S(2)}) collective-permute-start(bf16[128,896]{1,0:T(8,128)(2,1)S(1)} %get-tuple-element.48), channel_id=1, source_target_pairs={{0,1},{1,2},{2,3},{3,4},{4,5},{5,6},{6,7},{7,0},{8,9},{9,10},{10,1... | collective-permute-start | bytes 688136 | tf_op jit(solution)/shard_map/ppermute | solution.py:165
  4.6 9.3 %collective-permute-start.5 = (bf16[128,896]{1,0:T(8,128)(2,1)S(1)}, bf16[128,896]{1,0:T(8,128)(2,1)S(1)}, u32[]{:S(2)}, u32[]{:S(2)}) collective-permute-start(bf16[128,896]{1,0:T(8,128)(2,1)S(1)} %get-tuple-element.48), channel_id=1, source_target_pairs={{0,7},{1,0},{2,1},{3,2},{4,3},{5,4},{6,5},{7,6},{8,15},{9,8},{10,9... | collective-permute-start | bytes 688136 | tf_op jit(solution)/shard_map/ppermute | solution.py:166
  8.8 8.4 %collective-permute-start = (bf16[128,1024]{1,0:T(8,128)(2,1)S(1)}, bf16[128,1024]{1,0:T(8,128)(2,1)S(1)}, u32[]{:S(2)}, u32[]{:S(2)}) collective-permute-start(bf16[128,1024]{1,0:T(8,128)(2,1)S(1)} %pad_maximum_fusion.3), channel_id=1, source_target_pairs={{0,8},{1,9},{2,10},{3,11},{4,12},{5,13},{6,14},{7,15},{8,0},{9,1},... | collective-permute-start | bytes 786440 | tf_op jit(solution)/shard_map/ppermute | solution.py:150
  11.6 13.6 %collective-permute-start.3 = (bf16[64,2048]{1,0:T(8,128)(2,1)S(1)}, bf16[64,2048]{1,0:T(8,128)(2,1)S(1)}, u32[]{:S(2)}, u32[]{:S(2)}) collective-permute-start(bf16[64,2048]{1,0:T(8,128)(2,1)S(1)} %constant_dynamic-slice_fusion), channel_id=1, source_target_pairs={{0,8},{1,9},{2,10},{3,11},{4,12},{5,13},{6,14},{7,15},{8,0},{9,1},... | collective-permute-start | bytes 786440 | tf_op jit(solution)/shard_map/ppermute | solution.py:139
  13.9 7.1 %collective-permute-start.6 = (bf16[128,896]{1,0:T(8,128)(2,1)S(1)}, bf16[128,896]{1,0:T(8,128)(2,1)S(1)}, u32[]{:S(2)}, u32[]{:S(2)}) collective-permute-start(bf16[128,896]{1,0:T(8,128)(2,1)S(1)} %collective-permute-done.4), channel_id=1, source_target_pairs={{0,1},{1,2},{2,3},{3,4},{4,5},{5,6},{6,7},{7,0},{8,9},{9,10},{10,1... | collective-permute-start | bytes 688136 | tf_op jit(solution)/shard_map/ppermute | solution.py:165
  13.9 7.1 %collective-permute-start.7 = (bf16[128,896]{1,0:T(8,128)(2,1)S(1)}, bf16[128,896]{1,0:T(8,128)(2,1)S(1)}, u32[]{:S(2)}, u32[]{:S(2)}) collective-permute-start(bf16[128,896]{1,0:T(8,128)(2,1)S(1)} %collective-permute-done.5), channel_id=1, source_target_pairs={{0,7},{1,0},{2,1},{3,2},{4,3},{5,4},{6,5},{7,6},{8,15},{9,8},{10,9... | collective-permute-start | bytes 688136 | tf_op jit(solution)/shard_map/ppermute | solution.py:166
  17.2 8.0 %collective-permute-start.1 = (bf16[128,896]{1,0:T(8,128)(2,1)S(1)}, bf16[128,896]{1,0:T(8,128)(2,1)S(1)}, u32[]{:S(2)}, u32[]{:S(2)}) collective-permute-start(bf16[128,896]{1,0:T(8,128)(2,1)S(1)} %slice.69), channel_id=1, source_target_pairs={{0,1},{1,2},{2,3},{3,4},{4,5},{5,6},{6,7},{7,0},{8,9},{9,10},{10,1... | collective-permute-start | bytes 688136 | tf_op jit(solution)/shard_map/ppermute | solution.py:165
  17.3 7.9 %collective-permute-start.2 = (bf16[128,896]{1,0:T(8,128)(2,1)S(1)}, bf16[128,896]{1,0:T(8,128)(2,1)S(1)}, u32[]{:S(2)}, u32[]{:S(2)}) collective-permute-start(bf16[128,896]{1,0:T(8,128)(2,1)S(1)} %slice.69), channel_id=1, source_target_pairs={{0,7},{1,0},{2,1},{3,2},{4,3},{5,4},{6,5},{7,6},{8,15},{9,8},{10,9... | collective-permute-start | bytes 688136 | tf_op jit(solution)/shard_map/ppermute | solution.py:166
  20.9 12.4 %collective-permute-start.8 = (bf16[128,896]{1,0:T(8,128)(2,1)S(1)}, bf16[128,896]{1,0:T(8,128)(2,1)S(1)}, u32[]{:S(2)}, u32[]{:S(2)}) collective-permute-start(bf16[128,896]{1,0:T(8,128)(2,1)S(1)} %collective-permute-done.6), channel_id=1, source_target_pairs={{0,1},{1,2},{2,3},{3,4},{4,5},{5,6},{6,7},{7,0},{8,9},{9,10},{10,1... | collective-permute-start | bytes 688136 | tf_op jit(solution)/shard_map/ppermute | solution.py:165
  21.8 11.5 %collective-permute-start.9 = (bf16[128,896]{1,0:T(8,128)(2,1)S(1)}, bf16[128,896]{1,0:T(8,128)(2,1)S(1)}, u32[]{:S(2)}, u32[]{:S(2)}) collective-permute-start(bf16[128,896]{1,0:T(8,128)(2,1)S(1)} %collective-permute-done.7), channel_id=1, source_target_pairs={{0,7},{1,0},{2,1},{3,2},{4,3},{5,4},{6,5},{7,6},{8,15},{9,8},{10,9... | collective-permute-start | bytes 688136 | tf_op jit(solution)/shard_map/ppermute | solution.py:166
  25.2 16.0 %collective-permute-start.10 = (bf16[64,2048]{1,0:T(8,128)(2,1)S(1)}, bf16[64,2048]{1,0:T(8,128)(2,1)S(1)}, u32[]{:S(2)}, u32[]{:S(2)}) collective-permute-start(bf16[64,2048]{1,0:T(8,128)(2,1)S(1)} %collective-permute-done.3), channel_id=1, source_target_pairs={{0,16},{16,0},{32,48},{48,32},{64,80},{80,64},{96,112},{112,96},{1... | collective-permute-start | bytes 786440 | tf_op jit(solution)/shard_map/ppermute | solution.py:172
  30.4 8.5 %collective-permute-start.11 = (bf16[128,896]{1,0:T(8,128)(2,1)S(1)}, bf16[128,896]{1,0:T(8,128)(2,1)S(1)}, u32[]{:S(2)}, u32[]{:S(2)}) collective-permute-start(bf16[128,896]{1,0:T(8,128)(2,1)S(1)} %collective-permute-done.1), channel_id=1, source_target_pairs={{0,1},{1,2},{2,3},{3,4},{4,5},{5,6},{6,7},{7,0},{8,9},{9,10},{10,1... | collective-permute-start | bytes 688136 | tf_op jit(solution)/shard_map/ppermute | solution.py:165
  31.9 7.1 %collective-permute-start.12 = (bf16[128,896]{1,0:T(8,128)(2,1)S(1)}, bf16[128,896]{1,0:T(8,128)(2,1)S(1)}, u32[]{:S(2)}, u32[]{:S(2)}) collective-permute-start(bf16[128,896]{1,0:T(8,128)(2,1)S(1)} %collective-permute-done.2), channel_id=1, source_target_pairs={{0,7},{1,0},{2,1},{3,2},{4,3},{5,4},{6,5},{7,6},{8,15},{9,8},{10,9... | collective-permute-start | bytes 688136 | tf_op jit(solution)/shard_map/ppermute | solution.py:166
  39.0 6.2 %collective-permute-start.14 = (bf16[128,896]{1,0:T(8,128)(2,1)S(1)}, bf16[128,896]{1,0:T(8,128)(2,1)S(1)}, u32[]{:S(2)}, u32[]{:S(2)}) collective-permute-start(bf16[128,896]{1,0:T(8,128)(2,1)S(1)} %collective-permute-done.12), channel_id=1, source_target_pairs={{0,7},{1,0},{2,1},{3,2},{4,3},{5,4},{6,5},{7,6},{8,15},{9,8},{10,9... | collective-permute-start | bytes 688136 | tf_op jit(solution)/shard_map/ppermute | solution.py:166
  41.3 7.5 %collective-permute-start.13 = (bf16[128,896]{1,0:T(8,128)(2,1)S(1)}, bf16[128,896]{1,0:T(8,128)(2,1)S(1)}, u32[]{:S(2)}, u32[]{:S(2)}) collective-permute-start(bf16[128,896]{1,0:T(8,128)(2,1)S(1)} %collective-permute-done.11), channel_id=1, source_target_pairs={{0,1},{1,2},{2,3},{3,4},{4,5},{5,6},{6,7},{7,0},{8,9},{9,10},{10,1... | collective-permute-start | bytes 688136 | tf_op jit(solution)/shard_map/ppermute | solution.py:165
  41.3 11.8 %collective-permute-start.15 = (bf16[128,896]{1,0:T(8,128)(2,1)S(1)}, bf16[128,896]{1,0:T(8,128)(2,1)S(1)}, u32[]{:S(2)}, u32[]{:S(2)}) collective-permute-start(bf16[128,896]{1,0:T(8,128)(2,1)S(1)} %collective-permute-done.8), channel_id=1, source_target_pairs={{0,1},{1,2},{2,3},{3,4},{4,5},{5,6},{6,7},{7,0},{8,9},{9,10},{10,1... | collective-permute-start | bytes 688136 | tf_op jit(solution)/shard_map/ppermute | solution.py:179
  45.2 8.8 %collective-permute-start.16 = (bf16[128,896]{1,0:T(8,128)(2,1)S(1)}, bf16[128,896]{1,0:T(8,128)(2,1)S(1)}, u32[]{:S(2)}, u32[]{:S(2)}) collective-permute-start(bf16[128,896]{1,0:T(8,128)(2,1)S(1)} %collective-permute-done.14), channel_id=1, source_target_pairs={{0,7},{1,0},{2,1},{3,2},{4,3},{5,4},{6,5},{7,6},{8,15},{9,8},{10,9... | collective-permute-start | bytes 688136 | tf_op jit(solution)/shard_map/ppermute | solution.py:180
  55.6 14.9 %all-to-all-start = ((bf16[16,8,1024]{2,1,0:T(8,128)(2,1)}), bf16[16,8,1024]{2,1,0:T(8,128)(2,1)S(1)}, u32[]{:S(2)}, u32[]{:S(2)}) async-start(bf16[16,8,1024]{2,1,0:T(8,128)(2,1)} %fusion.14), calls=%async_computation | async-start | bytes 524288 | tf_op jit(solution)/shard_map/all_to_all | solution.py:206
  71.2 16.5 %all-to-all-start.1 = ((bf16[16,8,1024]{2,1,0:T(8,128)(2,1)}), bf16[16,8,1024]{2,1,0:T(8,128)(2,1)S(1)}, u32[]{:S(2)}, u32[]{:S(2)}) async-start(bf16[16,8,1024]{2,1,0:T(8,128)(2,1)} %broadcast_in_dim.101), calls=%async_computation.1 | async-start | bytes 524288 | tf_op jit(solution)/shard_map/all_to_all | solution.py:127
  78.6 16.9 %collective-permute-start.17 = (f32[128,1024]{1,0:T(8,128)S(1)}, f32[128,1024]{1,0:T(8,128)S(1)}, u32[]{:S(2)}, u32[]{:S(2)}) collective-permute-start(f32[128,1024]{1,0:T(8,128)S(1)} %pad_maximum_fusion.1), channel_id=1, source_target_pairs={{0,8},{1,9},{2,10},{3,11},{4,12},{5,13},{6,14},{7,15},{8,0},{9,1},... | collective-permute-start | bytes 1572872 | tf_op jit(solution)/shard_map/ppermute | solution.py:225
  89.1 16.0 %all-to-all-start.2 = ((bf16[16,8,1920]{2,1,0:T(8,128)(2,1)}), bf16[16,8,1920]{2,1,0:T(8,128)(2,1)S(1)}, u32[]{:S(2)}, u32[]{:S(2)}) async-start(bf16[16,8,1920]{2,1,0:T(8,128)(2,1)} %broadcast_in_dim.104), calls=%async_computation.2 | async-start | bytes 983040 | tf_op jit(solution)/shard_map/all_to_all | solution.py:127
  105.1 0.8 copy-start.1

commit v4 on v3

--- a/solution.py
+++ b/solution.py
@@ -24,12 +24,21 @@
 
 
 def correlate_kernel(
-    channel_ref, source_ref, out_ref, turned_ref, left_ref, right_ref, stage_ref, sems
+    channel_ref,
+    far_ref,
+    out_ref,
+    source_ref,
+    turned_ref,
+    left_ref,
+    right_ref,
+    stage_ref,
+    sems,
+    source_sem,
 ):
     rows = source_ref.shape[0]
     channels, samples = channel_ref.shape
-    scales = source_ref[:, samples:].astype(jnp.float32)
-    scale = (scales[:, :1] + scales[:, 127:]) * (1.0 / float(samples) ** 0.5)
+    arriving = pltpu.make_async_copy(far_ref, source_ref, source_sem)
+    arriving.start()
     turned_ref[:SPAN, :] = jnp.zeros((SPAN, channels), jnp.float32)
     turned_ref[SPAN + samples :, :] = jnp.zeros((SPAN, channels), jnp.float32)
     turned_ref[SPAN : SPAN + samples, :] = channel_ref[...].astype(jnp.float32).T
@@ -69,8 +78,11 @@
                 )
         return made
 
+    place_channels(0)
+    arriving.wait()
+    scales = source_ref[:, samples:].astype(jnp.float32)
+    scale = (scales[:, :1] + scales[:, 127:]) * (1.0 / float(samples) ** 0.5)
     place_sources(0)
-    place_channels(0)
     for side in range(2):
         for begin in range(0, FINE, CHUNK):
             some = min(CHUNK, FINE - begin)
@@ -105,14 +117,16 @@
     return pl.pallas_call(
         correlate_kernel,
         out_shape=jax.ShapeDtypeStruct((ROUNDS, LAGS, SRC, channels), jnp.bfloat16),
-        in_specs=[pl.BlockSpec(memory_space=pltpu.VMEM)] * 2,
+        in_specs=[pl.BlockSpec(memory_space=pltpu.VMEM), pl.BlockSpec(memory_space=pl.ANY)],
         out_specs=pl.BlockSpec(memory_space=pl.ANY),
         scratch_shapes=[
+            pltpu.VMEM(sources.shape, sources.dtype),
             pltpu.VMEM((samples + 2 * SPAN, channels), jnp.float32),
             pltpu.VMEM((2, FINE * rows, samples), jnp.bfloat16),
             pltpu.VMEM((2, samples, COARSE * channels), jnp.bfloat16),
             pltpu.VMEM((2, ROUNDS, SPAN, SRC, channels), jnp.bfloat16),
             pltpu.SemaphoreType.DMA((2, ROUNDS)),
+            pltpu.SemaphoreType.DMA,
         ],
         compiler_params=pltpu.CompilerParams(vmem_limit_bytes=56 * 2**20),
         cost_estimate=pl.CostEstimate(
@@ -164,7 +178,7 @@
         for who in range(2):
             one = lax.ppermute(up[who], "grp", UP)
             two = lax.ppermute(down[who], "grp", DOWN)
-            if hop < 3 or who == 0:
+            if hop < 3:
                 one, two = lax.optimization_barrier((one, two))
             up[who], down[who] = one, two
             if hop == 1 and who == 1:

time: 122 us -> 124 us (1.016)
  waiting for transfers between devices: 35.9 us -> 38.4 us
    ppermute x1, waiting for transfers between devices: 4.09 us -> 0.55 us  [on_device(): held.append((DEPTH // 2, 0, lax.ppermute(up[0], 'grp', UP)))]
    ppermute x6, waiting for transfers between devices: 0.21 us -> 3.01 us  [on_device(): two = lax.ppermute(down[who], 'grp', DOWN)]
    ppermute x6, waiting for transfers between devices: 9.33 us -> 11 us  [on_device(): one = lax.ppermute(up[who], 'grp', UP)]
    ppermute x1, waiting for transfers between devices: 0.01 us -> 1.62 us  [on_device(): held.append((DEPTH // 2, 1, lax.ppermute(down[1], 'grp', DOWN)))]
    ppermute x6, starting transfers between devices: 5.07 us -> 3.54 us  [on_device(): one = lax.ppermute(up[who], 'grp', UP)]
where the time goes in v4:
time: 124 us; the launch traced here: 123 us
  starting transfers between devices  55.3 us (45%)
  waiting for transfers between devices  38.4 us (31%)
  Pallas kernels  15.8 us (13%)
  matrix products  5.93 us (5%)
  other arithmetic  4.31 us (3%)
  local copies, waits for them, and re-layouts  2.96 us (2%)
    pallas_call x1, Pallas kernels, correlate(): pl.pallas_call(correlate_kernel, out_shape=jax.ShapeDtypeStruct((ROUNDS,...  15.8 us
    all_to_all x2, starting transfers between devices, everyone(): return lax.all_to_all(tiled, axis, 0, 0)  14.8 us
    all_to_all x2, waiting for transfers between devices, everyone(): return lax.all_to_all(tiled, axis, 0, 0)  14.6 us
    ppermute x6, starting transfers between devices, on_device(): two = lax.ppermute(down[who], 'grp', DOWN)  14.5 us
    ppermute x6, waiting for transfers between devices, on_device(): one = lax.ppermute(up[who], 'grp', UP)  11 us
    all_to_all x1, starting transfers between devices, on_device(): spread_rows = jnp.sum(lax.all_to_all(picked, 'seg', 0, 0), axis=0)  7.54 us
    all_to_all x1, waiting for transfers between devices, on_device(): spread_rows = jnp.sum(lax.all_to_all(picked, 'seg', 0, 0), axis=0)  6.99 us
    ppermute x1, starting transfers between devices, on_device(): handed = lax.ppermute(fetched, 'seg', CORES)  5.18 us
  transfers between devices with their start and end apart: 21, of which 11 were waited for; matrix products, arithmetic and copies ran while one was open for 7% of the time, Pallas kernels for 0%

profile of v4, /device:TPU:1, one launch (start us, length us, event | category | flops | bytes accessed | tf_op | source)
XLA Modules:
  0.0 123.3 jit_solution(17192775619318860275)
XLA Ops:
  0.0 0.7 broadcast_shift-right-arithmetic_fusion.1
  0.8 1.2 fusion.15
  2.0 2.5 %collective-permute-start.4 = (bf16[128,896]{1,0:T(8,128)(2,1)S(1)}, bf16[128,896]{1,0:T(8,128)(2,1)S(1)}, u32[]{:S(2)}, u32[]{:S(2)}) collective-permute-start(bf16[128,896]{1,0:T(8,128)(2,1)S(1)} %get-tuple-element.44), channel_id=1, source_target_pairs={{0,1},{1,2},{2,3},{3,4},{4,5},{5,6},{6,7},{7,0},{8,9},{9,10},{10,1... | collective-permute-start | bytes 688136 | tf_op jit(solution)/shard_map/ppermute | solution.py:179
  4.6 4.0 %collective-permute-start.5 = (bf16[128,896]{1,0:T(8,128)(2,1)S(1)}, bf16[128,896]{1,0:T(8,128)(2,1)S(1)}, u32[]{:S(2)}, u32[]{:S(2)}) collective-permute-start(bf16[128,896]{1,0:T(8,128)(2,1)S(1)} %get-tuple-element.44), channel_id=1, source_target_pairs={{0,7},{1,0},{2,1},{3,2},{4,3},{5,4},{6,5},{7,6},{8,15},{9,8},{10,9... | collective-permute-start | bytes 688136 | tf_op jit(solution)/shard_map/ppermute | solution.py:180
  8.8 2.8 %collective-permute-start = (bf16[128,1024]{1,0:T(8,128)(2,1)S(1)}, bf16[128,1024]{1,0:T(8,128)(2,1)S(1)}, u32[]{:S(2)}, u32[]{:S(2)}) collective-permute-start(bf16[128,1024]{1,0:T(8,128)(2,1)S(1)} %pad_maximum_fusion.3), channel_id=1, source_target_pairs={{0,8},{1,9},{2,10},{3,11},{4,12},{5,13},{6,14},{7,15},{8,0},{9,1},... | collective-permute-start | bytes 786440 | tf_op jit(solution)/shard_map/ppermute | solution.py:164
  11.6 0.3 collective-permute-start.3
  12.5 1.4 %collective-permute-done.4 = bf16[128,896]{1,0:T(8,128)(2,1)S(1)} collective-permute-done((bf16[128,896]{1,0:T(8,128)(2,1)S(1)}, bf16[128,896]{1,0:T(8,128)(2,1)S(1)}, u32[]{:S(2)}, u32[]{:S(2)}) %collective-permute-start.4) | collective-permute-done | bytes 229408 | tf_op jit(solution)/shard_map/ppermute | solution.py:179
  13.9 2.7 %collective-permute-start.7 = (bf16[128,896]{1,0:T(8,128)(2,1)S(1)}, bf16[128,896]{1,0:T(8,128)(2,1)S(1)}, u32[]{:S(2)}, u32[]{:S(2)}) collective-permute-start(bf16[128,896]{1,0:T(8,128)(2,1)S(1)} %collective-permute-done.5), channel_id=1, source_target_pairs={{0,7},{1,0},{2,1},{3,2},{4,3},{5,4},{6,5},{7,6},{8,15},{9,8},{10,9... | collective-permute-start | bytes 688136 | tf_op jit(solution)/shard_map/ppermute | solution.py:180
  16.5 0.7 collective-permute-done
  17.3 2.7 %collective-permute-start.2 = (bf16[128,896]{1,0:T(8,128)(2,1)S(1)}, bf16[128,896]{1,0:T(8,128)(2,1)S(1)}, u32[]{:S(2)}, u32[]{:S(2)}) collective-permute-start(bf16[128,896]{1,0:T(8,128)(2,1)S(1)} %slice.69), channel_id=1, source_target_pairs={{0,7},{1,0},{2,1},{3,2},{4,3},{5,4},{6,5},{7,6},{8,15},{9,8},{10,9... | collective-permute-start | bytes 688136 | tf_op jit(solution)/shard_map/ppermute | solution.py:180
  20.2 0.8 collective-permute-done.6
  20.9 0.9 collective-permute-start.8
  21.8 3.4 %collective-permute-done.1 = bf16[128,896]{1,0:T(8,128)(2,1)S(1)} collective-permute-done((bf16[128,896]{1,0:T(8,128)(2,1)S(1)}, bf16[128,896]{1,0:T(8,128)(2,1)S(1)}, u32[]{:S(2)}, u32[]{:S(2)}) %collective-permute-start.1) | collective-permute-done | bytes 229408 | tf_op jit(solution)/shard_map/ppermute | solution.py:179
  25.2 5.2 %collective-permute-start.9 = (bf16[64,2048]{1,0:T(8,128)(2,1)S(1)}, bf16[64,2048]{1,0:T(8,128)(2,1)S(1)}, u32[]{:S(2)}, u32[]{:S(2)}) collective-permute-start(bf16[64,2048]{1,0:T(8,128)(2,1)S(1)} %collective-permute-done.3), channel_id=1, source_target_pairs={{0,16},{16,0},{32,48},{48,32},{64,80},{80,64},{96,112},{112,96},{1... | collective-permute-start | bytes 786440 | tf_op jit(solution)/shard_map/ppermute | solution.py:186
  30.4 2.7 %collective-permute-start.11 = (bf16[128,896]{1,0:T(8,128)(2,1)S(1)}, bf16[128,896]{1,0:T(8,128)(2,1)S(1)}, u32[]{:S(2)}, u32[]{:S(2)}) collective-permute-start(bf16[128,896]{1,0:T(8,128)(2,1)S(1)} %collective-permute-done.2), channel_id=1, source_target_pairs={{0,7},{1,0},{2,1},{3,2},{4,3},{5,4},{6,5},{7,6},{8,15},{9,8},{10,9... | collective-permute-start | bytes 688136 | tf_op jit(solution)/shard_map/ppermute | solution.py:180
  33.3 5.5 %collective-permute-done.10 = bf16[128,896]{1,0:T(8,128)(2,1)S(1)} collective-permute-done((bf16[128,896]{1,0:T(8,128)(2,1)S(1)}, bf16[128,896]{1,0:T(8,128)(2,1)S(1)}, u32[]{:S(2)}, u32[]{:S(2)}) %collective-permute-start.10) | collective-permute-done | bytes 229408 | tf_op jit(solution)/shard_map/ppermute | solution.py:179
  38.8 2.3 %collective-permute-start.14 = (bf16[128,896]{1,0:T(8,128)(2,1)S(1)}, bf16[128,896]{1,0:T(8,128)(2,1)S(1)}, u32[]{:S(2)}, u32[]{:S(2)}) collective-permute-start(bf16[128,896]{1,0:T(8,128)(2,1)S(1)} %collective-permute-done.11), channel_id=1, source_target_pairs={{0,7},{1,0},{2,1},{3,2},{4,3},{5,4},{6,5},{7,6},{8,15},{9,8},{10,9... | collective-permute-start | bytes 688136 | tf_op jit(solution)/shard_map/ppermute | solution.py:180
  41.5 0.3 fusion.36
  41.8 0.3 fusion.38
  42.1 0.3 fusion.40
  42.4 0.3 fusion.42
  42.6 0.3 fusion.44
  42.9 0.3 fusion.46
  43.2 0.3 fusion.48
  43.4 0.3 fusion.54
  43.7 0.3 convolution_add_fusion.2
  44.0 0.3 fusion.50
  44.3 0.3 fusion.34
  44.5 3.0 %collective-permute-done.14 = bf16[128,896]{1,0:T(8,128)(2,1)S(1)} collective-permute-done((bf16[128,896]{1,0:T(8,128)(2,1)S(1)}, bf16[128,896]{1,0:T(8,128)(2,1)S(1)}, u32[]{:S(2)}, u32[]{:S(2)}) %collective-permute-start.14) | collective-permute-done | bytes 229408 | tf_op jit(solution)/shard_map/ppermute | solution.py:180
  47.5 3.4 %collective-permute-start.16 = (bf16[128,896]{1,0:T(8,128)(2,1)S(1)}, bf16[128,896]{1,0:T(8,128)(2,1)S(1)}, u32[]{:S(2)}, u32[]{:S(2)}) collective-permute-start(bf16[128,896]{1,0:T(8,128)(2,1)S(1)} %collective-permute-done.14), channel_id=1, source_target_pairs={{0,7},{1,0},{2,1},{3,2},{4,3},{5,4},{6,5},{7,6},{8,15},{9,8},{10,9... | collective-permute-start | bytes 688136 | tf_op jit(solution)/shard_map/ppermute | solution.py:194
  51.2 0.3 fusion.32
  51.5 0.6 collective-permute-done.15
  52.3 0.7 fusion.13
  53.0 1.6 %collective-permute-done.16 = bf16[128,896]{1,0:T(8,128)(2,1)S(1)} collective-permute-done((bf16[128,896]{1,0:T(8,128)(2,1)S(1)}, bf16[128,896]{1,0:T(8,128)(2,1)S(1)}, u32[]{:S(2)}, u32[]{:S(2)}) %collective-permute-start.16) | collective-permute-done | bytes 229408 | tf_op jit(solution)/shard_map/ppermute | solution.py:194
  54.6 0.5 fusion.77
  55.1 1.0 fusion.14
  56.1 7.5 %all-to-all-start = ((bf16[16,8,1024]{2,1,0:T(8,128)(2,1)}), bf16[16,8,1024]{2,1,0:T(8,128)(2,1)S(1)}, u32[]{:S(2)}, u32[]{:S(2)}) async-start(bf16[16,8,1024]{2,1,0:T(8,128)(2,1)} %fusion.14), calls=%async_computation | async-start | bytes 524288 | tf_op jit(solution)/shard_map/all_to_all | solution.py:220
  63.8 7.0 %all-to-all-done = bf16[16,8,1024]{2,1,0:T(8,128)(2,1)S(1)} async-done(((bf16[16,8,1024]{2,1,0:T(8,128)(2,1)}), bf16[16,8,1024]{2,1,0:T(8,128)(2,1)S(1)}, u32[]{:S(2)}, u32[]{:S(2)}) %all-to-all-start) | async-done | bytes 262176 | tf_op jit(solution)/shard_map/all_to_all | solution.py:220
  70.9 0.7 broadcast_in_dim.101
  71.6 8.3 %all-to-all-start.1 = ((bf16[16,8,1024]{2,1,0:T(8,128)(2,1)}), bf16[16,8,1024]{2,1,0:T(8,128)(2,1)S(1)}, u32[]{:S(2)}, u32[]{:S(2)}) async-start(bf16[16,8,1024]{2,1,0:T(8,128)(2,1)} %broadcast_in_dim.101), calls=%async_computation.1 | async-start | bytes 524288 | tf_op jit(solution)/shard_map/all_to_all | solution.py:141
  80.1 3.0 %collective-permute-start.17 = (f32[128,1024]{1,0:T(8,128)S(1)}, f32[128,1024]{1,0:T(8,128)S(1)}, u32[]{:S(2)}, u32[]{:S(2)}) collective-permute-start(f32[128,1024]{1,0:T(8,128)S(1)} %pad_maximum_fusion.1), channel_id=1, source_target_pairs={{0,8},{1,9},{2,10},{3,11},{4,12},{5,13},{6,14},{7,15},{8,0},{9,1},... | collective-permute-start | bytes 1572872 | tf_op jit(solution)/shard_map/ppermute | solution.py:239
  83.1 6.2 %all-to-all-done.1 = bf16[16,8,1024]{2,1,0:T(8,128)(2,1)S(1)} async-done(((bf16[16,8,1024]{2,1,0:T(8,128)(2,1)}), bf16[16,8,1024]{2,1,0:T(8,128)(2,1)S(1)}, u32[]{:S(2)}, u32[]{:S(2)}) %all-to-all-start.1) | async-done | bytes 262176 | tf_op jit(solution)/shard_map/all_to_all | solution.py:141
  89.7 0.8 broadcast_in_dim.104
  90.6 6.5 %all-to-all-start.2 = ((bf16[16,8,1920]{2,1,0:T(8,128)(2,1)}), bf16[16,8,1920]{2,1,0:T(8,128)(2,1)S(1)}, u32[]{:S(2)}, u32[]{:S(2)}) async-start(bf16[16,8,1920]{2,1,0:T(8,128)(2,1)} %broadcast_in_dim.104), calls=%async_computation.2 | async-start | bytes 983040 | tf_op jit(solution)/shard_map/all_to_all | solution.py:141
  97.3 0.8 pad_maximum_fusion.2.channel_ref
  98.1 8.4 %all-to-all-done.2 = bf16[16,8,1920]{2,1,0:T(8,128)(2,1)S(1)} async-done(((bf16[16,8,1920]{2,1,0:T(8,128)(2,1)}), bf16[16,8,1920]{2,1,0:T(8,128)(2,1)S(1)}, u32[]{:S(2)}, u32[]{:S(2)}) %all-to-all-start.2) | async-done | bytes 491552 | tf_op jit(solution)/shard_map/all_to_all | solution.py:141
  106.6 0.8 copy-done.1
  107.3 15.8 %shard_map.64 = bf16[2,201,64,128]{3,2,1,0:T(8,128)(2,1)} custom-call(bf16[128,1792]{1,0:T(8,128)(2,1)} %pad_maximum_fusion.2.channel_ref, bf16[128,1920]{1,0:T(8,128)(2,1)} %bitcast.28), custom_call_target="tpu_custom_call" | custom-call | flops 11802771456 | bytes 8388608 | tf_op jit(solution)/shard_map/pallas_call | solution.py:117
  (61 shorter events, 3.2 us)
Async XLA Ops:
  0.0 11.6 %copy-start = (bf16[128,2048]{1,0:T(8,128)(2,1)S(1)}, bf16[128,2048]{1,0:T(8,128)(2,1)}, u32[]{:S(2)}) copy-start(bf16[128,2048]{1,0:T(8,128)(2,1)} %param.9) | copy-start | bytes 1572868
  0.0 11.9 %copy-start.2 = (s32[2]{0:T(128)S(1)}, s32[2]{0:T(128)}, u32[]{:S(2)}) copy-start(s32[2]{0:T(128)} %param.11) | copy-start | bytes 28
  0.0 12.1 %copy-start.3 = (s32[2]{0:T(128)S(1)}, s32[2]{0:T(128)}, u32[]{:S(2)}) copy-start(s32[2]{0:T(128)} %param.10) | copy-start | bytes 28
  2.0 11.8 %collective-permute-start.4 = (bf16[128,896]{1,0:T(8,128)(2,1)S(1)}, bf16[128,896]{1,0:T(8,128)(2,1)S(1)}, u32[]{:S(2)}, u32[]{:S(2)}) collective-permute-start(bf16[128,896]{1,0:T(8,128)(2,1)S(1)} %get-tuple-element.44), channel_id=1, source_target_pairs={{0,1},{1,2},{2,3},{3,4},{4,5},{5,6},{6,7},{7,0},{8,9},{9,10},{10,1... | collective-permute-start | bytes 688136 | tf_op jit(solution)/shard_map/ppermute | solution.py:179
  4.6 9.3 %collective-permute-start.5 = (bf16[128,896]{1,0:T(8,128)(2,1)S(1)}, bf16[128,896]{1,0:T(8,128)(2,1)S(1)}, u32[]{:S(2)}, u32[]{:S(2)}) collective-permute-start(bf16[128,896]{1,0:T(8,128)(2,1)S(1)} %get-tuple-element.44), channel_id=1, source_target_pairs={{0,7},{1,0},{2,1},{3,2},{4,3},{5,4},{6,5},{7,6},{8,15},{9,8},{10,9... | collective-permute-start | bytes 688136 | tf_op jit(solution)/shard_map/ppermute | solution.py:180
  8.8 8.4 %collective-permute-start = (bf16[128,1024]{1,0:T(8,128)(2,1)S(1)}, bf16[128,1024]{1,0:T(8,128)(2,1)S(1)}, u32[]{:S(2)}, u32[]{:S(2)}) collective-permute-start(bf16[128,1024]{1,0:T(8,128)(2,1)S(1)} %pad_maximum_fusion.3), channel_id=1, source_target_pairs={{0,8},{1,9},{2,10},{3,11},{4,12},{5,13},{6,14},{7,15},{8,0},{9,1},... | collective-permute-start | bytes 786440 | tf_op jit(solution)/shard_map/ppermute | solution.py:164
  11.6 13.6 %collective-permute-start.3 = (bf16[64,2048]{1,0:T(8,128)(2,1)S(1)}, bf16[64,2048]{1,0:T(8,128)(2,1)S(1)}, u32[]{:S(2)}, u32[]{:S(2)}) collective-permute-start(bf16[64,2048]{1,0:T(8,128)(2,1)S(1)} %constant_dynamic-slice_fusion), channel_id=1, source_target_pairs={{0,8},{1,9},{2,10},{3,11},{4,12},{5,13},{6,14},{7,15},{8,0},{9,1},... | collective-permute-start | bytes 786440 | tf_op jit(solution)/shard_map/ppermute | solution.py:153
  13.9 7.1 %collective-permute-start.6 = (bf16[128,896]{1,0:T(8,128)(2,1)S(1)}, bf16[128,896]{1,0:T(8,128)(2,1)S(1)}, u32[]{:S(2)}, u32[]{:S(2)}) collective-permute-start(bf16[128,896]{1,0:T(8,128)(2,1)S(1)} %collective-permute-done.4), channel_id=1, source_target_pairs={{0,1},{1,2},{2,3},{3,4},{4,5},{5,6},{6,7},{7,0},{8,9},{9,10},{10,1... | collective-permute-start | bytes 688136 | tf_op jit(solution)/shard_map/ppermute | solution.py:179
  13.9 7.1 %collective-permute-start.7 = (bf16[128,896]{1,0:T(8,128)(2,1)S(1)}, bf16[128,896]{1,0:T(8,128)(2,1)S(1)}, u32[]{:S(2)}, u32[]{:S(2)}) collective-permute-start(bf16[128,896]{1,0:T(8,128)(2,1)S(1)} %collective-permute-done.5), channel_id=1, source_target_pairs={{0,7},{1,0},{2,1},{3,2},{4,3},{5,4},{6,5},{7,6},{8,15},{9,8},{10,9... | collective-permute-start | bytes 688136 | tf_op jit(solution)/shard_map/ppermute | solution.py:180
  17.2 8.0 %collective-permute-start.1 = (bf16[128,896]{1,0:T(8,128)(2,1)S(1)}, bf16[128,896]{1,0:T(8,128)(2,1)S(1)}, u32[]{:S(2)}, u32[]{:S(2)}) collective-permute-start(bf16[128,896]{1,0:T(8,128)(2,1)S(1)} %slice.69), channel_id=1, source_target_pairs={{0,1},{1,2},{2,3},{3,4},{4,5},{5,6},{6,7},{7,0},{8,9},{9,10},{10,1... | collective-permute-start | bytes 688136 | tf_op jit(solution)/shard_map/ppermute | solution.py:179
  17.3 7.9 %collective-permute-start.2 = (bf16[128,896]{1,0:T(8,128)(2,1)S(1)}, bf16[128,896]{1,0:T(8,128)(2,1)S(1)}, u32[]{:S(2)}, u32[]{:S(2)}) collective-permute-start(bf16[128,896]{1,0:T(8,128)(2,1)S(1)} %slice.69), channel_id=1, source_target_pairs={{0,7},{1,0},{2,1},{3,2},{4,3},{5,4},{6,5},{7,6},{8,15},{9,8},{10,9... | collective-permute-start | bytes 688136 | tf_op jit(solution)/shard_map/ppermute | solution.py:180
  20.9 20.2 %collective-permute-start.8 = (bf16[128,896]{1,0:T(8,128)(2,1)S(1)}, bf16[128,896]{1,0:T(8,128)(2,1)S(1)}, u32[]{:S(2)}, u32[]{:S(2)}) collective-permute-start(bf16[128,896]{1,0:T(8,128)(2,1)S(1)} %collective-permute-done.6), channel_id=1, source_target_pairs={{0,1},{1,2},{2,3},{3,4},{4,5},{5,6},{6,7},{7,0},{8,9},{9,10},{10,1... | collective-permute-start | bytes 688136 | tf_op jit(solution)/shard_map/ppermute | solution.py:179
  25.2 15.9 %collective-permute-start.9 = (bf16[64,2048]{1,0:T(8,128)(2,1)S(1)}, bf16[64,2048]{1,0:T(8,128)(2,1)S(1)}, u32[]{:S(2)}, u32[]{:S(2)}) collective-permute-start(bf16[64,2048]{1,0:T(8,128)(2,1)S(1)} %collective-permute-done.3), channel_id=1, source_target_pairs={{0,16},{16,0},{32,48},{48,32},{64,80},{80,64},{96,112},{112,96},{1... | collective-permute-start | bytes 786440 | tf_op jit(solution)/shard_map/ppermute | solution.py:186
  30.4 8.4 %collective-permute-start.10 = (bf16[128,896]{1,0:T(8,128)(2,1)S(1)}, bf16[128,896]{1,0:T(8,128)(2,1)S(1)}, u32[]{:S(2)}, u32[]{:S(2)}) collective-permute-start(bf16[128,896]{1,0:T(8,128)(2,1)S(1)} %collective-permute-done.1), channel_id=1, source_target_pairs={{0,1},{1,2},{2,3},{3,4},{4,5},{5,6},{6,7},{7,0},{8,9},{9,10},{10,1... | collective-permute-start | bytes 688136 | tf_op jit(solution)/shard_map/ppermute | solution.py:179
  30.4 8.4 %collective-permute-start.11 = (bf16[128,896]{1,0:T(8,128)(2,1)S(1)}, bf16[128,896]{1,0:T(8,128)(2,1)S(1)}, u32[]{:S(2)}, u32[]{:S(2)}) collective-permute-start(bf16[128,896]{1,0:T(8,128)(2,1)S(1)} %collective-permute-done.2), channel_id=1, source_target_pairs={{0,7},{1,0},{2,1},{3,2},{4,3},{5,4},{6,5},{7,6},{8,15},{9,8},{10,9... | collective-permute-start | bytes 688136 | tf_op jit(solution)/shard_map/ppermute | solution.py:180
  33.2 11.0 %collective-permute-start.12 = (bf16[128,896]{1,0:T(8,128)(2,1)S(1)}, bf16[128,896]{1,0:T(8,128)(2,1)S(1)}, u32[]{:S(2)}, u32[]{:S(2)}) collective-permute-start(bf16[128,896]{1,0:T(8,128)(2,1)S(1)} %collective-permute-done.7), channel_id=1, source_target_pairs={{0,7},{1,0},{2,1},{3,2},{4,3},{5,4},{6,5},{7,6},{8,15},{9,8},{10,9... | collective-permute-start | bytes 688136 | tf_op jit(solution)/shard_map/ppermute | solution.py:180
  38.8 8.7 %collective-permute-start.14 = (bf16[128,896]{1,0:T(8,128)(2,1)S(1)}, bf16[128,896]{1,0:T(8,128)(2,1)S(1)}, u32[]{:S(2)}, u32[]{:S(2)}) collective-permute-start(bf16[128,896]{1,0:T(8,128)(2,1)S(1)} %collective-permute-done.11), channel_id=1, source_target_pairs={{0,7},{1,0},{2,1},{3,2},{4,3},{5,4},{6,5},{7,6},{8,15},{9,8},{10,9... | collective-permute-start | bytes 688136 | tf_op jit(solution)/shard_map/ppermute | solution.py:180
  41.1 10.1 %collective-permute-start.13 = (bf16[128,896]{1,0:T(8,128)(2,1)S(1)}, bf16[128,896]{1,0:T(8,128)(2,1)S(1)}, u32[]{:S(2)}, u32[]{:S(2)}) collective-permute-start(bf16[128,896]{1,0:T(8,128)(2,1)S(1)} %collective-permute-done.10), channel_id=1, source_target_pairs={{0,1},{1,2},{2,3},{3,4},{4,5},{5,6},{6,7},{7,0},{8,9},{9,10},{10,1... | collective-permute-start | bytes 688136 | tf_op jit(solution)/shard_map/ppermute | solution.py:179
  41.1 10.9 %collective-permute-start.15 = (bf16[128,896]{1,0:T(8,128)(2,1)S(1)}, bf16[128,896]{1,0:T(8,128)(2,1)S(1)}, u32[]{:S(2)}, u32[]{:S(2)}) collective-permute-start(bf16[128,896]{1,0:T(8,128)(2,1)S(1)} %collective-permute-done.8), channel_id=1, source_target_pairs={{0,1},{1,2},{2,3},{3,4},{4,5},{5,6},{6,7},{7,0},{8,9},{9,10},{10,1... | collective-permute-start | bytes 688136 | tf_op jit(solution)/shard_map/ppermute | solution.py:193
  47.5 7.1 %collective-permute-start.16 = (bf16[128,896]{1,0:T(8,128)(2,1)S(1)}, bf16[128,896]{1,0:T(8,128)(2,1)S(1)}, u32[]{:S(2)}, u32[]{:S(2)}) collective-permute-start(bf16[128,896]{1,0:T(8,128)(2,1)S(1)} %collective-permute-done.14), channel_id=1, source_target_pairs={{0,7},{1,0},{2,1},{3,2},{4,3},{5,4},{6,5},{7,6},{8,15},{9,8},{10,9... | collective-permute-start | bytes 688136 | tf_op jit(solution)/shard_map/ppermute | solution.py:194
  56.1 14.7 %all-to-all-start = ((bf16[16,8,1024]{2,1,0:T(8,128)(2,1)}), bf16[16,8,1024]{2,1,0:T(8,128)(2,1)S(1)}, u32[]{:S(2)}, u32[]{:S(2)}) async-start(bf16[16,8,1024]{2,1,0:T(8,128)(2,1)} %fusion.14), calls=%async_computation | async-start | bytes 524288 | tf_op jit(solution)/shard_map/all_to_all | solution.py:220
  71.6 17.7 %all-to-all-start.1 = ((bf16[16,8,1024]{2,1,0:T(8,128)(2,1)}), bf16[16,8,1024]{2,1,0:T(8,128)(2,1)S(1)}, u32[]{:S(2)}, u32[]{:S(2)}) async-start(bf16[16,8,1024]{2,1,0:T(8,128)(2,1)} %broadcast_in_dim.101), calls=%async_computation.1 | async-start | bytes 524288 | tf_op jit(solution)/shard_map/all_to_all | solution.py:141
  80.1 16.9 %collective-permute-start.17 = (f32[128,1024]{1,0:T(8,128)S(1)}, f32[128,1024]{1,0:T(8,128)S(1)}, u32[]{:S(2)}, u32[]{:S(2)}) collective-permute-start(f32[128,1024]{1,0:T(8,128)S(1)} %pad_maximum_fusion.1), channel_id=1, source_target_pairs={{0,8},{1,9},{2,10},{3,11},{4,12},{5,13},{6,14},{7,15},{8,0},{9,1},... | collective-permute-start | bytes 1572872 | tf_op jit(solution)/shard_map/ppermute | solution.py:239
  90.6 16.0 %all-to-all-start.2 = ((bf16[16,8,1920]{2,1,0:T(8,128)(2,1)}), bf16[16,8,1920]{2,1,0:T(8,128)(2,1)S(1)}, u32[]{:S(2)}, u32[]{:S(2)}) async-start(bf16[16,8,1920]{2,1,0:T(8,128)(2,1)} %broadcast_in_dim.104), calls=%async_computation.2 | async-start | bytes 983040 | tf_op jit(solution)/shard_map/all_to_all | solution.py:141
  106.6 0.8 copy-start.1
